TPU v7x, 32 devices: a whole 2x2x4 slice. The times are simulated.
32 devices in a mesh: shot: 8 (over z, y), rcv: 4 (over x, core).
Axes of the slice: x: 2, y: 2, z: 4, core: 2. Of those that a mesh axis runs over, the one named last changes fastest.
Arguments:
- record: bfloat16 [8192, 2048], P('shot', 'rcv'), may hold values from -6 to 6
- offsets: int32 [8], P('shot'), may hold values from 0 to 1023
- lengths: int32 [8], P('shot'), may hold values from 1024 to 2048
- thresholds: float32 [3], replicated, may hold values from 0.05 to 0.5
Outputs:
- estimate: float32 [8, 2048, 2048], P('shot', None, 'rcv')
All inputs are finite; a program needn't handle non-finite values.
Results may differ from a plain program's by a relative error of at most 0.0003.
Values sent between devices are 32-bit elements; how exact they have to be, the bound alone decides.
No kernel may reach another device: no remote copies, remote signals or barrier semaphores. Data moves between devices by JAX's collectives and lax.ppermute only.
A program may use at most 64 MiB of HBM per device.

v0:
```python
import functools

import numpy as np
import jax
import jax.numpy as jnp
from jax import lax
from jax.experimental import pallas as pl
from jax.experimental.pallas import tpu as pltpu
from jax.sharding import PartitionSpec as P

LEVELS = 3
relax_step = 0.5

PLANES = 5
LANES = 128
RING = PLANES * LANES
HALF = LANES // 2
EDGE = 32
QUARTERS = LANES // EDGE
HEAD = 128
PAD = 64
ROWHALO = 16
BLOCK = 64
STRIP = 64


def shifted(shard, axis, by):
    devices = lax.axis_size(axis)
    pairs = [(i, i + by) for i in range(devices) if 0 <= i + by < devices]
    return lax.ppermute(shard, axis, pairs)


def ring_matrices(columns):
    wide = columns + 2 * LANES
    into = np.zeros((wide, RING), np.float32)
    back = np.zeros((RING, columns), np.float32)

    def place(ring):
        pair, side = divmod(ring, 2)
        return (pair % PLANES) * LANES + side * HALF + pair // PLANES

    for column in range(columns):
        into[column, place(EDGE + column)] = relax_step
        back[place(EDGE + column), column] = 1.0
    for quarter in range(LANES // EDGE):
        for i in range(EDGE):
            into[columns + quarter * EDGE + i, place(i)] = relax_step
            into[columns + LANES + quarter * EDGE + i, place(EDGE + columns + i)] = relax_step
    return jnp.asarray(into, jnp.bfloat16), jnp.asarray(back, jnp.bfloat16)


def smooth_across(planes, dilation):
    if dilation == 1:
        lane = lax.broadcasted_iota(jnp.int32, planes[0].shape, 1)
        other = [pltpu.roll(x, HALF, 1) for x in planes]
        before = [pltpu.roll(planes[-1], HALF + 1, 1)] + other[:-1]
        after = other[1:] + [pltpu.roll(planes[0], HALF - 1, 1)]
        two_before = [pltpu.roll(planes[-1], 1, 1)] + planes[:-1]
        two_after = planes[1:] + [pltpu.roll(planes[0], LANES - 1, 1)]
        return [
            (two_before[k] + two_after[k])
            + 4.0 * (other[k] + jnp.where(lane < HALF, before[k], after[k]))
            + 6.0 * planes[k]
            for k in range(PLANES)
        ]
    rolled = {}
    pairs = dilation // 2

    def at(position):
        turns, plane = divmod(position, PLANES)
        if turns == 0:
            return planes[plane]
        if (turns, plane) not in rolled:
            rolled[turns, plane] = pltpu.roll(planes[plane], (-turns) % LANES, 1)
        return rolled[turns, plane]

    return [
        (at(k - 2 * pairs) + at(k + 2 * pairs)) + 4.0 * (at(k - pairs) + at(k + pairs)) + 6.0 * planes[k]
        for k in range(PLANES)
    ]


def limit(values, cut):
    return jnp.minimum(jnp.maximum(values, -cut), cut)


def blocks_of(first, count, body):
    def step(b, carry):
        body(pl.multiple_of(first + b * (2 * BLOCK), 8), 2 * BLOCK)
        return carry

    lax.fori_loop(0, count // 2, step, 0)
    pl.when(count % 2 == 1)(lambda: body(pl.multiple_of(first + (count - 1) * BLOCK, 8), BLOCK))


def smooth_block(ref, start, rows, dilation, scale):
    centre, summed = [], []
    for k in range(PLANES):
        x = [ref[k, pl.ds(start + tap * dilation, rows), :] for tap in range(-2, 3)]
        centre.append(x[2])
        summed.append((x[0] + x[4]) + 4.0 * (x[1] + x[3]) + 6.0 * x[2])
    summed = smooth_across(summed, dilation)
    return centre, [s * w for s, w in zip(summed, scale)]


def deblend_kernel(geometry, pieces, halo_places, outers, span, operands, params, thr, *refs):
    seg, columns = geometry
    into_hbm, back_hbm, *sources = refs[:operands]
    out, into, back, ext, halos, beyond, gathered, c1, c2, f, strip, staged, sem, out_sem = refs[operands:]
    window = 2 * seg
    quarter_rows = seg // QUARTERS

    shots = lax.axis_size("shot")
    me = lax.axis_index("shot")
    rcv = lax.axis_index("rcv")
    offset = params[2, 0]
    live = params[2, 1]
    total = (shots - me) * seg - offset

    def shot(by):
        return by * seg + params[by + 2, 0] - offset, params[by + 2, 1]

    spans = [(pl.multiple_of(begin * BLOCK, 8), jnp.maximum(end - begin, 0)) for begin, end in span(offset)]
    some = sum(count for _, count in spans) > 0

    def reached(row, rows):
        found = False
        for low, count in spans:
            inside = (row < offset + low + count * BLOCK + 40) & (row + rows > offset + low - 40)
            found = found | ((count > 0) & inside)
        return found

    def copy_of(n, src, target):
        return pltpu.make_async_copy(src, target, sem.at[n])

    brought = [(0, None, into, some)]
    for main, first, rows, row in pieces:
        brought.append((main, (first, rows), ext.at[pl.ds(row, rows), :], reached(row, rows)))
    for segment, place in enumerate(halo_places):
        if place is not None:
            brought.append((place, (0, HEAD), halos.at[segment], some))
    for n, (place, row) in enumerate(outers):
        brought.append((place, (0, ROWHALO), beyond.at[n], reached(row, ROWHALO)))

    pl.when(some)(lambda: copy_of(0, into_hbm, into).start())
    for n, (place, part, target, wanted) in enumerate(brought):
        if part is not None:
            pl.when(wanted)(lambda: copy_of(n, sources[place].at[pl.ds(*part), :], target).start())
    pl.when(some)(lambda: copy_of(len(brought), back_hbm, back).start())

    lane = lax.broadcasted_iota(jnp.int32, (1, LANES), 1)
    has_right = jnp.where(rcv < lax.axis_size("rcv") - 1, 1.0, 0.0)
    has_left = jnp.where(rcv > 0, 1.0, 0.0)
    scale = []
    for k in range(PLANES):
        ring = 2 * (lane % HALF * PLANES + k) + lane // HALF
        side = jnp.where(ring < EDGE, has_left, has_right)
        scale.append(jnp.where((ring >= EDGE) & (ring < EDGE + columns), 1.0, side) * (1.0 / 256.0))
    strip[:, :, 0:16, :] = jnp.zeros((3, PLANES, 16, LANES), jnp.float32)
    strip[:, :, 16 + STRIP : 32 + STRIP, :] = jnp.zeros((3, PLANES, 16, LANES), jnp.float32)

    for n, (place, part, target, wanted) in enumerate(brought):
        pl.when(wanted)(lambda: copy_of(n, target, target).wait())

    def permute_in(main, left, right, quarter, row):
        mine = (lane // EDGE) == quarter
        lhs = [main] + [jnp.where(mine, x, 0.0) for x in (left, right)]
        lhs = jnp.concatenate([x.astype(jnp.bfloat16) for x in lhs], axis=1)
        result = jnp.dot(lhs, into[...], preferred_element_type=jnp.float32)
        for k in range(PLANES):
            gathered[0, k, pl.ds(PAD + row, main.shape[0]), :] = result[:, k * LANES : (k + 1) * LANES]

    def permute_quarter(i, carry):
        row = pl.multiple_of(i * quarter_rows, quarter_rows)
        segment = row // seg
        sides = []
        for side in range(2):
            lanes = [2 * side * LANES + at // HEAD * LANES for at in range(0, quarter_rows, HEAD)]
            sides.append(jnp.concatenate([halos[segment, :, at : at + LANES] for at in lanes], axis=0))
        permute_in(ext[pl.ds(row, quarter_rows), :], *sides, lax.rem(row, seg) // quarter_rows, row)
        return carry

    for low, count in spans:
        begin = jnp.clip((offset + low - 40) // quarter_rows, 0, 3 * QUARTERS)
        end = jnp.clip((offset + low + count * BLOCK + 40 + quarter_rows - 1) // quarter_rows, 0, 3 * QUARTERS)
        lax.fori_loop(begin, jnp.where(count > 0, end, begin), permute_quarter, 0)
    for n, (place, row) in enumerate(outers):

        @pl.when(reached(row, ROWHALO))
        def _():
            sides = [beyond[n, :, columns + side * LANES : columns + (side + 1) * LANES] for side in range(2)]
            permute_in(beyond[n, :, 0:columns], *sides, QUARTERS - 1 if row < 0 else 0, row)

    def level_pass(source, shift, target, dilation, first, count):
        def body(at, rows):
            _, summed = smooth_block(source, at + shift, rows, dilation, scale)
            for k in range(PLANES):
                target[k, pl.ds(at, rows), :] = summed[k]

        blocks_of(first, count, body)

    def shrunk(sweep, shift, at, rows):
        centre, summed = smooth_block(c2, at, rows, 4, scale)
        for k in range(PLANES):
            x0 = gathered[sweep, k, pl.ds(at + shift, rows), :]
            x1 = c1[k, pl.ds(at, rows), :]
            x2 = centre[k]
            clipped = limit(x0 - x1, thr[0]) + limit(x1 - x2, thr[1]) + limit(x2 - summed[k], thr[2])
            yield k, x0, x0 - clipped

    def next_gathered(at, rows):
        t = at - PAD + lax.broadcasted_iota(jnp.int32, (rows, LANES), 0)
        shots_live = jnp.zeros(t.shape, jnp.float32)
        for by in range(-2, 3):
            begin, length = shot(by)
            shots_live = shots_live + jnp.where((t >= begin) & (t < begin + length), 1.0, 0.0)
        own_live = jnp.where((t >= 0) & (t < live), 1.0, 0.0)
        inside = jnp.where(t < total, relax_step, 0.0)
        factor = own_live * (1.0 - inside * shots_live)
        for k, x0, value in shrunk(0, offset, at, rows):
            f[k, pl.ds(at, rows), :] = value
            gathered[1, k, pl.ds(at, rows), :] = own_live * x0 + factor * value

    half = STRIP // 2

    def do_strip(by, at_end):
        begin, length = shot(by)
        p = begin + jnp.where(at_end, length, 0)
        t = p - half + lax.broadcasted_iota(jnp.int32, (STRIP, LANES), 0)
        in_live = jnp.where((t >= begin) & (t < begin + length), 1.0, 0.0)
        in_window = jnp.where((t >= begin) & (t < begin + window), 1.0, 0.0)
        for k in range(PLANES):
            strip[0, k, 16 : 16 + STRIP, :] = gathered[0, k, pl.ds(PAD + offset + p - half, STRIP), :] * in_live
        for j in range(2):
            _, summed = smooth_block(strip.at[j], 16, STRIP, 2**j, scale)
            for k in range(PLANES):
                strip[j + 1, k, 16 : 16 + STRIP, :] = summed[k] * in_window
        mid = half
        _, summed = smooth_block(strip.at[2], mid, 32, 4, scale)
        t = p - 16 + lax.broadcasted_iota(jnp.int32, (32, LANES), 0)
        in_window = jnp.where((t >= begin) & (t < begin + window), 1.0, 0.0)
        near_edge = (t >= begin) & (t < begin + length) & (t >= p - 14) & (t < p + 14)
        own_live = (t >= 0) & (t < live)
        inside = jnp.where(t < total, -relax_step, 0.0)
        weight = jnp.where(near_edge & own_live, inside + jnp.where(by == 0, 1.0, 0.0), 0.0)
        for k in range(PLANES):
            x0 = strip[0, k, mid : mid + 32, :]
            x1 = strip[1, k, mid : mid + 32, :]
            x2 = strip[2, k, mid : mid + 32, :]
            x3 = summed[k] * in_window
            clipped = limit(x0 - x1, thr[0]) + limit(x1 - x2, thr[1]) + limit(x2 - x3, thr[2])
            where = pl.ds(PAD + p - 16, 32)
            gathered[1, k, where, :] = gathered[1, k, where, :] + weight * (x0 - clipped - f[k, where, :])

    def out_copy(block):
        rows = pl.ds(pl.multiple_of(block * BLOCK, BLOCK), BLOCK)
        return pltpu.make_async_copy(staged.at[rows, :], out.at[0, rows, :], out_sem.at[block])

    def estimate(at, rows):
        t = at - PAD + lax.broadcasted_iota(jnp.int32, (rows, LANES), 0)
        own_live = jnp.where(t < live, 1.0, 0.0)
        high, rest = [], []
        for k, _, value in shrunk(1, 0, at, rows):
            x = own_live * value
            h = x.astype(jnp.bfloat16)
            high.append(h)
            rest.append((x - h.astype(jnp.float32)).astype(jnp.bfloat16))
        both = jnp.concatenate([jnp.concatenate(high, axis=1), jnp.concatenate(rest, axis=1)], axis=0)
        result = jnp.dot(both, back[...], preferred_element_type=jnp.float32)
        staged[pl.ds(pl.multiple_of(at - PAD, 8), rows), :] = result[:rows] + result[rows:]
        for n in range(rows // BLOCK):
            out_copy((at - PAD) // BLOCK + n).start()

    def clear_edges(ref):
        ref[:, PAD - 16 : PAD, :] = jnp.zeros((PLANES, 16, LANES), jnp.float32)
        ref[:, PAD + window : PAD + window + 16, :] = jnp.zeros((PLANES, 16, LANES), jnp.float32)

    def process(low, count):
        high = low + count * BLOCK
        first = PAD + low
        wider, many = first - BLOCK // 2, count + 1

        def strip_step(i, carry):
            by, at_end = i // 2 - 2, i % 2 == 1
            begin, length = shot(by)
            p = begin + jnp.where(at_end, length, 0)
            begins_at = jnp.where(at_end, p - 14, p)
            bottom = jnp.maximum(low - 14, 0)
            top = jnp.minimum(high + 14, live)

            @pl.when((length > 0) & (begins_at + 14 > bottom) & (begins_at < top))
            def _():
                do_strip(by, at_end)

            return carry

        level_pass(gathered.at[0], offset, c1, 1, wider, many)
        level_pass(c1, 0, c2, 2, wider, many)
        blocks_of(wider, many, next_gathered)
        lax.fori_loop(1, 10, strip_step, 0)
        clear_edges(gathered.at[1])
        level_pass(gathered.at[1], 0, c1, 1, wider, many)
        clear_edges(c1)
        level_pass(c1, 0, c2, 2, wider, many)
        clear_edges(c2)
        blocks_of(first, count, estimate)

    pl.when(some)(lambda: copy_of(len(brought), back, back).wait())

    def span_step(i, carry):
        low, count = spans[0]
        if len(spans) > 1:
            low, count = jnp.where(i == 0, low, spans[1][0]), jnp.where(i == 0, count, spans[1][1])
        pl.when(count > 0)(lambda: process(pl.multiple_of(low, 8), count))
        return carry

    lax.fori_loop(0, len(spans), span_step, 0)

    def wait(i, carry):
        out_copy(i).wait()
        return carry

    for low, count in spans:
        lax.fori_loop(low // BLOCK, low // BLOCK + count, wait, 0)


def prepare_kernel(first_columns, last_columns, first_edge, last_edge):
    quarter = first_edge.shape[0]
    lane = lax.broadcasted_iota(jnp.int32, (1, LANES), 1)
    for out, source, inner in ((first_edge, first_columns, 0), (last_edge, last_columns, LANES - EDGE)):
        packed = jnp.zeros((quarter, LANES), jnp.float32)
        for q in range(QUARTERS):
            rows = source[q * quarter : (q + 1) * quarter, :].astype(jnp.float32)
            turn = (q * EDGE - inner) % LANES
            packed = jnp.where(lane // EDGE == q, pltpu.roll(rows, turn, 1) if turn else rows, packed)
        out[...] = packed


def header_kernel(offsets, lengths, first_rows, last_rows, left, right, own, wide_first, wide_last):
    quarter = left.shape[0]
    columns = own.shape[1]
    lane = lax.broadcasted_iota(jnp.int32, (8, LANES), 1)
    about = jnp.where(lane == 0, offsets[0], jnp.where(lane == 1, lengths[0], 0)).astype(jnp.float32)
    for side, halo in enumerate((left, right)):
        for part in range(quarter // HEAD):
            at = (2 * side + part) * LANES
            own[0:HEAD, at : at + LANES] = halo[part * HEAD : (part + 1) * HEAD, :]
    own[HEAD : HEAD + 8, :] = jnp.concatenate([about] * (columns // LANES), axis=1)
    own[HEAD + 8 :, :] = first_rows[...].astype(jnp.float32)
    wide_first[:, 0:columns] = first_rows[0:ROWHALO, :].astype(jnp.float32)
    wide_last[0:ROWHALO, 0:columns] = last_rows[...].astype(jnp.float32)
    for side, halo in enumerate((left, right)):
        at = columns + side * LANES
        wide_first[:, at : at + LANES] = halo[0:ROWHALO, :]
        wide_last[0:ROWHALO, at : at + LANES] = halo[quarter - ROWHALO : quarter, :]
    wide_last[ROWHALO:, :] = jnp.concatenate([about] * (columns // LANES + 2), axis=1)


def widen_kernel(begins, record, wait, *own):
    for begin, out in zip(begins, own):
        out[...] = record[begin : begin + out.shape[0], :].astype(jnp.float32)


def pass_on_kernel(unread, own, far, *refs):
    sent, sem = refs[unread], refs[-1]
    odd = lax.rem(lax.axis_index("shot"), 2) == 1
    pl.when(odd)(lambda: pltpu.make_async_copy(own, sent, sem).start())
    pl.when(jnp.logical_not(odd))(lambda: pltpu.make_async_copy(far, sent, sem).start())
    pltpu.make_async_copy(own, sent, sem).wait()


def shots_kernel(second_last, last, mine, following, second, out):
    lane = lax.broadcasted_iota(jnp.int32, (8, LANES), 1)
    row = lax.broadcasted_iota(jnp.int32, (8, LANES), 0)
    found = jnp.zeros((8, LANES), jnp.float32)
    for n, pair in enumerate((second_last, last, mine, following, second)):
        if n in (0, 2):
            value = jnp.where(lane == 0, pair[0], pair[1])
        else:
            value = pair[0:1, :]
        found = jnp.where(row == n, value, found)
    out[...] = found.astype(jnp.int32)


def on_device(record, offsets, lengths, thresholds):
    seg, columns = record.shape
    window = 2 * seg
    shots = lax.axis_size("shot")
    q = seg // QUARTERS
    skip = HEAD + 8
    step = (seg + skip + 4 * 16 - 1) // (4 * 16) * 16
    parts = [0] + [seg - k * step for k in (3, 2, 1, 0)]
    swap = [(i, i ^ 1) for i in range(shots) if i ^ 1 < shots]
    smem = pl.BlockSpec(memory_space=pltpu.SMEM)
    anywhere = pl.BlockSpec(memory_space=pl.ANY)
    vmem = pl.BlockSpec(memory_space=pltpu.VMEM)

    def array(*shape):
        return jax.ShapeDtypeStruct(shape, jnp.float32)

    def part(k):
        return array(parts[k + 1] - parts[k] + (skip if k == 0 else 0), columns)

    def window_of(rows, width, row, column):
        return pl.BlockSpec((rows, width), lambda _: (row, column))

    first_edge, last_edge = pl.pallas_call(
        prepare_kernel,
        grid=(1,),
        out_shape=(array(q, LANES), array(q, LANES)),
        in_specs=[window_of(seg, LANES, 0, 0), window_of(seg, LANES, 0, columns // LANES - 1)],
        out_specs=(vmem, vmem),
    )(record, record)
    from_left = shifted(last_edge, "rcv", 1)
    from_right = shifted(first_edge, "rcv", -1)
    mine = jnp.concatenate([offsets, lengths]).astype(jnp.float32)
    wide = columns + 2 * LANES
    first_part, wide_first, wide_last = pl.pallas_call(
        header_kernel,
        grid=(1,),
        out_shape=(part(0), array(ROWHALO, wide), array(ROWHALO + 8, wide)),
        in_specs=[smem, smem, window_of(parts[1], columns, 0, 0),
                  window_of(ROWHALO, columns, seg // ROWHALO - 1, 0), vmem, vmem],
        out_specs=(vmem,) * 3,
    )(offsets, lengths, record, record, from_left, from_right)
    swap = [(i, i ^ 1) for i in range(shots) if i ^ 1 < shots]
    far, near = [None] * 4, [None] * 4
    second_last = shifted(mine, "shot", 2)
    top = shifted(wide_last, "shot", 1)
    bot = shifted(wide_first, "shot", -3)
    far[0] = shifted(first_part, "shot", -2)
    own = [first_part] + list(pl.pallas_call(
        functools.partial(widen_kernel, parts[1:4]),
        out_shape=tuple(part(k) for k in (1, 2, 3)),
        in_specs=[vmem, anywhere],
        out_specs=(vmem,) * 3,
    )(record, top))
    far[1] = shifted(own[1], "shot", -2)

    def pass_on(k, *others):
        ahead = [own[k + 2]] if k + 2 < 4 else []
        sent, *ahead = pl.pallas_call(
            functools.partial(pass_on_kernel, len(ahead) + len(others)),
            out_shape=(part(k),) + tuple(array(*x.shape) for x in ahead),
            in_specs=[anywhere] * (2 + len(ahead) + len(others)),
            out_specs=(vmem,) + (anywhere,) * len(ahead),
            input_output_aliases={2: 1} if ahead else {},
            scratch_shapes=[pltpu.SemaphoreType.DMA],
        )(own[k], far[k], *ahead, *others)
        near[k] = lax.ppermute(sent, "shot", swap)
        if ahead:
            own[k + 2] = ahead[0]
            far[k + 2] = shifted(own[k + 2], "shot", -2)
        return sent

    pass_on(0)

    def corner(row):
        return pl.BlockSpec((8, LANES), lambda _: (row // 8, 0))

    params = pl.pallas_call(
        shots_kernel,
        grid=(1,),
        out_shape=jax.ShapeDtypeStruct((8, LANES), jnp.int32),
        in_specs=[smem, corner(ROWHALO), smem, corner(HEAD), corner(HEAD)],
        out_specs=vmem,
    )(second_last, top, mine, near[0], far[0])
    pass_on(1, params, bot)

    into, back = ring_matrices(columns)
    work = pltpu.VMEM((PLANES, window + 4 * PAD, LANES), jnp.float32)

    def phase(out, arrays, pieces, halo_places, outers, span):
        held = [] if out is None else [out]
        return pl.pallas_call(
            functools.partial(
                deblend_kernel, (seg, columns), pieces, halo_places, outers, span, 2 + len(arrays) + len(held)
            ),
            out_shape=array(1, window, columns),
            in_specs=[smem, smem] + [anywhere] * (2 + len(arrays) + len(held)),
            out_specs=anywhere,
            input_output_aliases={} if out is None else {4 + len(arrays): 0},
            scratch_shapes=[
                pltpu.VMEM(into.shape, into.dtype),
                pltpu.VMEM(back.shape, back.dtype),
                pltpu.VMEM((3 * seg, columns), jnp.float32),
                pltpu.VMEM((3, HEAD, columns), jnp.float32),
                pltpu.VMEM((2, ROWHALO, wide), jnp.float32),
                pltpu.VMEM((2, PLANES, 3 * seg + 4 * PAD, LANES), jnp.float32),
                work, work, work,
                pltpu.VMEM((3, PLANES, STRIP + 32, LANES), jnp.float32),
                pltpu.VMEM((window + BLOCK, columns), jnp.float32),
                pltpu.SemaphoreType.DMA((len(pieces) + 7,)),
                pltpu.SemaphoreType.DMA((window // BLOCK,)),
            ],
            compiler_params=pltpu.CompilerParams(vmem_limit_bytes=63 * 1024 * 1024),
        )(params, thresholds, into, back, *arrays, *held)

    def part_piece(k, main, segment):
        return (main, skip if k == 0 else 0, parts[k + 1] - parts[k], segment * seg + parts[k])

    blocks = window // BLOCK
    cap = 9

    def mark(offset, rows):
        return jnp.clip((seg + rows - 28 - offset) // BLOCK, 0, blocks)

    def far_begin(offset):
        return jnp.minimum((2 * seg + 35 - offset) // 8 * 8 // BLOCK, blocks)

    def far_middle(offset):
        return jnp.clip((2 * seg + parts[2] - 28 - offset) // BLOCK, far_begin(offset), blocks)

    def takes_far(offset):
        return far_middle(offset) - far_begin(offset) >= 4

    def first(offset):
        is_far = takes_far(offset)
        begin = jnp.where(is_far, far_begin(offset), 0)
        return [(begin, jnp.where(is_far, far_middle(offset), jnp.minimum(mark(offset, 0), cap)))]

    def second(offset):
        is_far = takes_far(offset)
        begin = jnp.where(is_far, 0, first(offset)[0][1])
        return [(begin, mark(offset, parts[2])), (jnp.where(is_far, far_middle(offset), far_begin(offset)), blocks)]

    def last(offset):
        bridged = (jnp.minimum((2 * seg + 35 - offset) // 8 * 8, window) + BLOCK - 1) // BLOCK
        return [(mark(offset, parts[2]), bridged)]

    def every(places, segment):
        return [part_piece(k, place, segment) for k, place in enumerate(places)]

    out = phase(
        None, [*own, top, far[0], far[1]], every(range(4), 0) + every((5, 6), 2), (0, None, 5), [(4, -ROWHALO)], first
    )
    pass_on(2, out)
    sent = pass_on(3)
    out = phase(
        out, [*far, *own, near[0], near[1], bot, top, sent],
        every(range(4), 2) + every(range(4, 8), 0) + every((8, 9), 1), (4, 8, 0),
        [(10, 3 * seg), (11, -ROWHALO)], second,
    )
    return phase(
        out, [own[0], own[3], *near, far[0], far[1]],
        [part_piece(3, 1, 0)] + every(range(2, 6), 1) + every((6, 7), 2), (0, 2, 6), [], last,
    )


def solution(mesh):
    return jax.shard_map(
        on_device,
        mesh=mesh,
        in_specs=(P("shot", "rcv"), P("shot"), P("shot"), P()),
        out_specs=P("shot", None, "rcv"),
        check_vma=False,
    )
```

profile of v0, /device:TPU:13, one launch (start us, length us, event | category | flops | bytes accessed | tf_op | source)
XLA Modules:
  0.0 118.0 jit_solution(1913025815033047956)
XLA Ops:
  0.0 1.9 %shard_map.64 = (f32[256,128]{1,0:T(8,128)}, f32[256,128]{1,0:T(8,128)}) custom-call(bf16[1024,512]{1,0:T(8,128)(2,1)} %record.1, bf16[1024,512]{1,0:T(8,128)(2,1)} %record.1), custom_call_target="tpu_custom_call" | custom-call | tf_op jit(solution)/shard_map/pallas_call | solution.py:407
  1.9 3.7 %collective-permute-start.1 = (f32[256,128]{1,0:T(8,128)}, f32[256,128]{1,0:T(8,128)S(1)}, u32[]{:S(2)}, u32[]{:S(2)}) collective-permute-start(f32[256,128]{1,0:T(8,128)} %get-tuple-element.17), channel_id=1, source_target_pairs={{0,1},{1,2},{2,3},{4,5},{5,6},{6,7},{8,9},{9,10},{10,11},{12,13},{... | collective-permute-start | bytes 393224 | tf_op jit(solution)/shard_map/ppermute | solution.py:30
  5.6 1.9 %collective-permute-start.2 = (f32[256,128]{1,0:T(8,128)}, f32[256,128]{1,0:T(8,128)S(1)}, u32[]{:S(2)}, u32[]{:S(2)}) collective-permute-start(f32[256,128]{1,0:T(8,128)} %get-tuple-element.18), channel_id=1, source_target_pairs={{1,0},{2,1},{3,2},{5,4},{6,5},{7,6},{9,8},{10,9},{11,10},{13,12},{... | collective-permute-start | bytes 393224 | tf_op jit(solution)/shard_map/ppermute | solution.py:30
  8.8 3.3 %collective-permute-done.2.right = f32[256,128]{1,0:T(8,128)S(1)} collective-permute-done((f32[256,128]{1,0:T(8,128)}, f32[256,128]{1,0:T(8,128)S(1)}, u32[]{:S(2)}, u32[]{:S(2)}) %collective-permute-start.2) | collective-permute-done | bytes 131104 | tf_op jit(solution)/shard_map/ppermute | solution.py:30
  12.1 0.7 copy-done.8
  12.7 1.9 %shard_map.65 = (f32[248,512]{1,0:T(8,128)}, f32[16,768]{1,0:T(8,128)}, f32[24,768]{1,0:T(8,128)}) custom-call(s32[1]{0:T(128)S(6)} %copy.15.offsets, s32[1]{0:T(128)S(6)} %copy.16.lengths, bf16[1024,512]{1,0:T(8,128)(2,1)} %record.1, bf16[1024,512]{1,0:T(8,128)(2,1)} %record.1, f32[256,128]{1,0:T(8,128)} %copy-done.7, f32[256,128]{1,0:T(8,128)} %copy-done.8), custom_call_target="tpu_custom_call" | custom-call | tf_op jit(solution)/shard_map/pallas_call | solution.py:418
  14.6 2.1 %collective-permute-start.4 = (f32[248,512]{1,0:T(8,128)}, f32[248,512]{1,0:T(8,128)S(1)}, u32[]{:S(2)}, u32[]{:S(2)}) collective-permute-start(f32[248,512]{1,0:T(8,128)} %get-tuple-element.20.own.refs_2_.refs_6_), channel_id=1, source_target_pairs={{8,0},{12,4},{16,8},{20,12},{24,16},{28,20},{9,1},{13,5},{17,9},{2... | collective-permute-start | bytes 1523720 | tf_op jit(solution)/shard_map/ppermute | solution.py:30
  16.7 3.1 %collective-permute-start.3 = (f32[24,768]{1,0:T(8,128)}, f32[24,768]{1,0:T(8,128)S(1)}, u32[]{:S(2)}, u32[]{:S(2)}) collective-permute-start(f32[24,768]{1,0:T(8,128)} %get-tuple-element.19), channel_id=1, source_target_pairs={{0,4},{4,8},{8,12},{12,16},{16,20},{20,24},{24,28},{1,5},{5,9},{9,... | collective-permute-start | bytes 221192 | tf_op jit(solution)/shard_map/ppermute | solution.py:30
  19.8 2.4 %collective-permute-done.3.wait.last.refs_6_.refs_13_ = f32[24,768]{1,0:T(8,128)S(1)} collective-permute-done((f32[24,768]{1,0:T(8,128)}, f32[24,768]{1,0:T(8,128)S(1)}, u32[]{:S(2)}, u32[]{:S(2)}) %collective-permute-start.3) | collective-permute-done | bytes 73760 | tf_op jit(solution)/shard_map/ppermute | solution.py:30
  22.9 2.6 %shard_map.66 = (f32[304,512]{1,0:T(8,128)}, f32[304,512]{1,0:T(8,128)}, f32[304,512]{1,0:T(8,128)}) custom-call(bf16[1024,512]{1,0:T(8,128)(2,1)} %record.1, f32[24,768]{1,0:T(8,128)} %copy-done.4), custom_call_target="tpu_custom_call" | custom-call | tf_op jit(solution)/shard_map/pallas_call | solution.py:432
  25.5 1.9 %collective-permute-start.6 = (f32[304,512]{1,0:T(8,128)}, f32[304,512]{1,0:T(8,128)S(1)}, u32[]{:S(2)}, u32[]{:S(2)}) collective-permute-start(f32[304,512]{1,0:T(8,128)} %get-tuple-element.23.own.refs_3_.refs_7_), channel_id=1, source_target_pairs={{8,0},{12,4},{16,8},{20,12},{24,16},{28,20},{9,1},{13,5},{17,9},{2... | collective-permute-start | bytes 1867784 | tf_op jit(solution)/shard_map/ppermute | solution.py:30
  27.4 0.8 copy-done
  28.2 1.8 %shard_map.67 = (f32[248,512]{1,0:T(8,128)}, f32[304,512]{1,0:T(8,128)}) custom-call(f32[248,512]{1,0:T(8,128)} %get-tuple-element.20.own.refs_2_.refs_6_, f32[248,512]{1,0:T(8,128)} %copy-done, f32[304,512]{1,0:T(8,128)} %get-tuple-element.21.refs_0_), custom_call_target="tpu_custom_call", output_to_operand_aliasing={{1}: (2, {})} | custom-call | tf_op jit(solution)/shard_map/pallas_call | solution.py:442
  30.1 0.9 collective-permute-start.5
  30.9 2.4 %collective-permute-start.7 = (f32[16,768]{1,0:T(8,128)}, f32[16,768]{1,0:T(8,128)S(1)}, u32[]{:S(2)}, u32[]{:S(2)}) collective-permute-start(f32[16,768]{1,0:T(8,128)} %get-tuple-element.25), channel_id=1, source_target_pairs={{12,0},{16,4},{20,8},{24,12},{28,16},{13,1},{17,5},{21,9},{25,13},... | collective-permute-start | bytes 147464 | tf_op jit(solution)/shard_map/ppermute | solution.py:30
  33.5 3.2 %collective-permute-start = (f32[2]{0:T(128)S(1)}, f32[2]{0:T(128)S(1)}, u32[]{:S(2)}, u32[]{:S(2)}) collective-permute-start(f32[2]{0:T(128)S(1)} %add_convert_fusion.mine), channel_id=1, source_target_pairs={{0,8},{4,12},{8,16},{12,20},{16,24},{20,28},{1,9},{5,13},{9,17},{1... | collective-permute-start | bytes 32 | tf_op jit(solution)/shard_map/ppermute | solution.py:30
  36.7 2.1 %collective-permute-start.9 = (f32[304,512]{1,0:T(8,128)}, f32[304,512]{1,0:T(8,128)}, u32[]{:S(2)}, u32[]{:S(2)}) collective-permute-start(f32[304,512]{1,0:T(8,128)} %get-tuple-element.28.refs_4_.own.refs_8_), channel_id=1, source_target_pairs={{8,0},{12,4},{16,8},{20,12},{24,16},{28,20},{9,1},{13,5},{17,9},{2... | collective-permute-start | bytes 1867784 | tf_op jit(solution)/shard_map/ppermute | solution.py:30
  38.8 3.8 %collective-permute-done.5.following.refs_10_.refs_4_ = f32[248,512]{1,0:T(8,128)S(1)} collective-permute-done((f32[248,512]{1,0:T(8,128)}, f32[248,512]{1,0:T(8,128)S(1)}, u32[]{:S(2)}, u32[]{:S(2)}) %collective-permute-start.5) | collective-permute-done | bytes 507936 | tf_op jit(solution)/shard_map/ppermute | solution.py:450
  42.6 0.8 copy-done.2
  43.4 1.4 %shard_map.68.refs_1_.params = s32[8,128]{1,0:T(8,128)} custom-call(f32[2]{0:T(128)} %copy-done.10, f32[24,768]{1,0:T(8,128)} %copy-done.4, f32[2]{0:T(128)} %copy-done.9, f32[248,512]{1,0:T(8,128)} %copy-done.2, f32[248,512]{1,0:T(8,128)} %copy-done), custom_call_target="tpu_custom_call" | custom-call | tf_op jit(solution)/shard_map/pallas_call | solution.py:461
  44.8 1.1 collective-permute-done.7.refs_2_.refs_12_
  46.8 1.9 %shard_map.69 = (f32[304,512]{1,0:T(8,128)}, f32[304,512]{1,0:T(8,128)}) custom-call(f32[304,512]{1,0:T(8,128)} %get-tuple-element.23.own.refs_3_.refs_7_, f32[304,512]{1,0:T(8,128)} %copy-done.1, f32[304,512]{1,0:T(8,128)} %get-tuple-element.24.refs_0_, s32[8,128]{1,0:T(8,128)} %shard_map.68.refs_1_.params, ...), custom_call_target="tpu_custom_call", output_to_operand_aliasing={{1}: (2, {})} | custom-call | tf_op jit(solution)/shard_map/pallas_call | solution.py:442
  48.8 3.1 %collective-permute-start.11 = (f32[304,512]{1,0:T(8,128)}, f32[304,512]{1,0:T(8,128)S(1)}, u32[]{:S(2)}, u32[]{:S(2)}) collective-permute-start(f32[304,512]{1,0:T(8,128)} %get-tuple-element.26.refs_5_.own.refs_9_.refs_3_), channel_id=1, source_target_pairs={{8,0},{12,4},{16,8},{20,12},{24,16},{28,20},{9,1},{13,5},{17,9},{2... | collective-permute-start | bytes 1867784 | tf_op jit(solution)/shard_map/ppermute | solution.py:30
  52.0 11.1 %shard_map.70.refs_0_.refs_15_ = f32[1,2048,512]{2,1,0:T(8,128)} custom-call(s32[8,128]{1,0:T(8,128)} %shard_map.68.refs_1_.params, f32[3]{0:T(128)} %thr.5, bf16[768,640]{1,0:T(8,128)(2,1)} %constant.4.clone.refs_0_, bf16[640,512]{1,0:T(8,128)(2,1)} %constant.5.clone.refs_1_, f32[248,512]{1,0:T(8,128)} %get-tuple-element.20.own.refs_2_.refs_6_, ...), custom_call_target="tpu_custom_call" | custom-call | tf_op jit(solution)/shard_map/pallas_call | solution.py:475
  63.1 1.9 %shard_map.71 = f32[304,512]{1,0:T(8,128)} custom-call(f32[304,512]{1,0:T(8,128)} %get-tuple-element.28.refs_4_.own.refs_8_, f32[304,512]{1,0:T(8,128)} %collective-permute-done.9.far.refs_4_, f32[1,2048,512]{2,1,0:T(8,128)} %shard_map.70.refs_0_.refs_15_), custom_call_target="tpu_custom_call" | custom-call | tf_op jit(solution)/shard_map/pallas_call | solution.py:442
  65.1 5.4 %collective-permute-start.10 = (f32[304,512]{1,0:T(8,128)}, f32[304,512]{1,0:T(8,128)}, u32[]{:S(2)}, u32[]{:S(2)}) collective-permute-start(f32[304,512]{1,0:T(8,128)} %shard_map.71), channel_id=1, source_target_pairs={{0,4},{4,0},{8,12},{12,8},{16,20},{20,16},{24,28},{28,24},{1,5},{5... | collective-permute-start | bytes 1867784 | tf_op jit(solution)/shard_map/ppermute | solution.py:450
  70.5 0.8 copy-done.3
  71.3 1.9 %shard_map.72.refs_14_ = f32[304,512]{1,0:T(8,128)} custom-call(f32[304,512]{1,0:T(8,128)} %get-tuple-element.26.refs_5_.own.refs_9_.refs_3_, f32[304,512]{1,0:T(8,128)} %copy-done.3), custom_call_target="tpu_custom_call" | custom-call | tf_op jit(solution)/shard_map/pallas_call | solution.py:442
  73.2 1.8 %collective-permute-start.12 = (f32[304,512]{1,0:T(8,128)}, f32[304,512]{1,0:T(8,128)S(1)}, u32[]{:S(2)}, u32[]{:S(2)}) collective-permute-start(f32[304,512]{1,0:T(8,128)} %shard_map.72.refs_14_), channel_id=1, source_target_pairs={{0,4},{4,0},{8,12},{12,8},{16,20},{20,16},{24,28},{28,24},{1,5},{5... | collective-permute-start | bytes 1867784 | tf_op jit(solution)/shard_map/ppermute | solution.py:450
  75.1 25.7 %shard_map.73.refs_10_ = f32[1,2048,512]{2,1,0:T(8,128)} custom-call(s32[8,128]{1,0:T(8,128)} %shard_map.68.refs_1_.params, f32[3]{0:T(128)} %thr.5, bf16[768,640]{1,0:T(8,128)(2,1)} %constant.4.clone.refs_0_, bf16[640,512]{1,0:T(8,128)(2,1)} %constant.5.clone.refs_1_, f32[248,512]{1,0:T(8,128)} %copy-done, ...), custom_call_target="tpu_custom_call", output_to_operand_aliasing={{}: (17, {})} | custom-call | tf_op jit(solution)/shard_map/pallas_call | solution.py:475
  100.8 0.8 copy-done.5
  101.6 16.4 %shard_map.74 = f32[1,2048,512]{2,1,0:T(8,128)} custom-call(s32[8,128]{1,0:T(8,128)} %shard_map.68.refs_1_.params, f32[3]{0:T(128)} %thr.5, bf16[768,640]{1,0:T(8,128)(2,1)} %constant.4.clone.refs_0_, bf16[640,512]{1,0:T(8,128)(2,1)} %constant.5.clone.refs_1_, f32[248,512]{1,0:T(8,128)} %get-tuple-element.20.own.refs_2_.refs_6_, ...), custom_call_target="tpu_custom_call", output_to_operand_aliasing={{}: (12, {})} | custom-call | tf_op jit(solution)/shard_map/pallas_call | solution.py:475
  (28 shorter events, 1.7 us)
Async XLA Ops:
  1.9 6.9 %collective-permute-start.1 = (f32[256,128]{1,0:T(8,128)}, f32[256,128]{1,0:T(8,128)S(1)}, u32[]{:S(2)}, u32[]{:S(2)}) collective-permute-start(f32[256,128]{1,0:T(8,128)} %get-tuple-element.17), channel_id=1, source_target_pairs={{0,1},{1,2},{2,3},{4,5},{5,6},{6,7},{8,9},{9,10},{10,11},{12,13},{... | collective-permute-start | bytes 393224 | tf_op jit(solution)/shard_map/ppermute | solution.py:30
  5.6 6.5 %collective-permute-start.2 = (f32[256,128]{1,0:T(8,128)}, f32[256,128]{1,0:T(8,128)S(1)}, u32[]{:S(2)}, u32[]{:S(2)}) collective-permute-start(f32[256,128]{1,0:T(8,128)} %get-tuple-element.18), channel_id=1, source_target_pairs={{1,0},{2,1},{3,2},{5,4},{6,5},{7,6},{9,8},{10,9},{11,10},{13,12},{... | collective-permute-start | bytes 393224 | tf_op jit(solution)/shard_map/ppermute | solution.py:30
  8.8 3.3 %copy-start.7 = (f32[256,128]{1,0:T(8,128)}, f32[256,128]{1,0:T(8,128)S(1)}, u32[]{:S(2)}) copy-start(f32[256,128]{1,0:T(8,128)S(1)} %collective-permute-done.1.left) | copy-start | bytes 393220
  12.1 0.7 copy-start.8
  14.6 12.8 %collective-permute-start.4 = (f32[248,512]{1,0:T(8,128)}, f32[248,512]{1,0:T(8,128)S(1)}, u32[]{:S(2)}, u32[]{:S(2)}) collective-permute-start(f32[248,512]{1,0:T(8,128)} %get-tuple-element.20.own.refs_2_.refs_6_), channel_id=1, source_target_pairs={{8,0},{12,4},{16,8},{20,12},{24,16},{28,20},{9,1},{13,5},{17,9},{2... | collective-permute-start | bytes 1523720 | tf_op jit(solution)/shard_map/ppermute | solution.py:30
  16.7 5.6 %collective-permute-start.3 = (f32[24,768]{1,0:T(8,128)}, f32[24,768]{1,0:T(8,128)S(1)}, u32[]{:S(2)}, u32[]{:S(2)}) collective-permute-start(f32[24,768]{1,0:T(8,128)} %get-tuple-element.19), channel_id=1, source_target_pairs={{0,4},{4,8},{8,12},{12,16},{16,20},{20,24},{24,28},{1,5},{5,9},{9,... | collective-permute-start | bytes 221192 | tf_op jit(solution)/shard_map/ppermute | solution.py:30
  22.3 0.6 copy-start.4
  25.5 20.5 %collective-permute-start.6 = (f32[304,512]{1,0:T(8,128)}, f32[304,512]{1,0:T(8,128)S(1)}, u32[]{:S(2)}, u32[]{:S(2)}) collective-permute-start(f32[304,512]{1,0:T(8,128)} %get-tuple-element.23.own.refs_3_.refs_7_), channel_id=1, source_target_pairs={{8,0},{12,4},{16,8},{20,12},{24,16},{28,20},{9,1},{13,5},{17,9},{2... | collective-permute-start | bytes 1867784 | tf_op jit(solution)/shard_map/ppermute | solution.py:30
  27.4 0.8 copy-start
  30.1 12.5 %collective-permute-start.5 = (f32[248,512]{1,0:T(8,128)}, f32[248,512]{1,0:T(8,128)S(1)}, u32[]{:S(2)}, u32[]{:S(2)}) collective-permute-start(f32[248,512]{1,0:T(8,128)} %get-tuple-element.22), channel_id=1, source_target_pairs={{0,4},{4,0},{8,12},{12,8},{16,20},{20,16},{24,28},{28,24},{1,5},{5... | collective-permute-start | bytes 1523720 | tf_op jit(solution)/shard_map/ppermute | solution.py:450
  30.9 15.0 %collective-permute-start.7 = (f32[16,768]{1,0:T(8,128)}, f32[16,768]{1,0:T(8,128)S(1)}, u32[]{:S(2)}, u32[]{:S(2)}) collective-permute-start(f32[16,768]{1,0:T(8,128)} %get-tuple-element.25), channel_id=1, source_target_pairs={{12,0},{16,4},{20,8},{24,12},{28,16},{13,1},{17,5},{21,9},{25,13},... | collective-permute-start | bytes 147464 | tf_op jit(solution)/shard_map/ppermute | solution.py:30
  33.5 9.1 %copy-start.9 = (f32[2]{0:T(128)}, f32[2]{0:T(128)S(1)}, u32[]{:S(2)}) copy-start(f32[2]{0:T(128)S(1)} %add_convert_fusion.mine) | copy-start | bytes 28
  33.5 5.3 %collective-permute-start = (f32[2]{0:T(128)S(1)}, f32[2]{0:T(128)S(1)}, u32[]{:S(2)}, u32[]{:S(2)}) collective-permute-start(f32[2]{0:T(128)S(1)} %add_convert_fusion.mine), channel_id=1, source_target_pairs={{0,8},{4,12},{8,16},{12,20},{16,24},{20,28},{1,9},{5,13},{9,17},{1... | collective-permute-start | bytes 32 | tf_op jit(solution)/shard_map/ppermute | solution.py:30
  36.7 26.5 %collective-permute-start.9 = (f32[304,512]{1,0:T(8,128)}, f32[304,512]{1,0:T(8,128)}, u32[]{:S(2)}, u32[]{:S(2)}) collective-permute-start(f32[304,512]{1,0:T(8,128)} %get-tuple-element.28.refs_4_.own.refs_8_), channel_id=1, source_target_pairs={{8,0},{12,4},{16,8},{20,12},{24,16},{28,20},{9,1},{13,5},{17,9},{2... | collective-permute-start | bytes 1867784 | tf_op jit(solution)/shard_map/ppermute | solution.py:30
  38.8 3.8 %copy-start.10 = (f32[2]{0:T(128)}, f32[2]{0:T(128)S(1)}, u32[]{:S(2)}) copy-start(f32[2]{0:T(128)S(1)} %collective-permute-done.second_last) | copy-start | bytes 28
  42.6 0.8 copy-start.2
  46.0 0.6 copy-start.6
  46.0 0.9 copy-start.1
  48.8 21.7 %collective-permute-start.11 = (f32[304,512]{1,0:T(8,128)}, f32[304,512]{1,0:T(8,128)S(1)}, u32[]{:S(2)}, u32[]{:S(2)}) collective-permute-start(f32[304,512]{1,0:T(8,128)} %get-tuple-element.26.refs_5_.own.refs_9_.refs_3_), channel_id=1, source_target_pairs={{8,0},{12,4},{16,8},{20,12},{24,16},{28,20},{9,1},{13,5},{17,9},{2... | collective-permute-start | bytes 1867784 | tf_op jit(solution)/shard_map/ppermute | solution.py:30
  51.9 23.1 %collective-permute-start.8 = (f32[304,512]{1,0:T(8,128)}, f32[304,512]{1,0:T(8,128)}, u32[]{:S(2)}, u32[]{:S(2)}) collective-permute-start(f32[304,512]{1,0:T(8,128)} %get-tuple-element.27), channel_id=1, source_target_pairs={{0,4},{4,0},{8,12},{12,8},{16,20},{20,16},{24,28},{28,24},{1,5},{5... | collective-permute-start | bytes 1867784 | tf_op jit(solution)/shard_map/ppermute | solution.py:450
  65.1 35.7 %collective-permute-start.10 = (f32[304,512]{1,0:T(8,128)}, f32[304,512]{1,0:T(8,128)}, u32[]{:S(2)}, u32[]{:S(2)}) collective-permute-start(f32[304,512]{1,0:T(8,128)} %shard_map.71), channel_id=1, source_target_pairs={{0,4},{4,0},{8,12},{12,8},{16,20},{20,16},{24,28},{28,24},{1,5},{5... | collective-permute-start | bytes 1867784 | tf_op jit(solution)/shard_map/ppermute | solution.py:450
  70.5 0.8 copy-start.3
  73.2 27.5 %collective-permute-start.12 = (f32[304,512]{1,0:T(8,128)}, f32[304,512]{1,0:T(8,128)S(1)}, u32[]{:S(2)}, u32[]{:S(2)}) collective-permute-start(f32[304,512]{1,0:T(8,128)} %shard_map.72.refs_14_), channel_id=1, source_target_pairs={{0,4},{4,0},{8,12},{12,8},{16,20},{20,16},{24,28},{28,24},{1,5},{5... | collective-permute-start | bytes 1867784 | tf_op jit(solution)/shard_map/ppermute | solution.py:450
  100.8 0.8 copy-start.5
where the time goes:
time: 119 us; the launch traced here: 118 us
  Pallas kernels  68.5 us (58%)
  starting transfers between devices  31.7 us (27%)
  waiting for transfers between devices  10.7 us (9%)
  local copies, waits for them, and re-layouts  5.49 us (5%)
  between operations  1.5 us (1%)
    pallas_call x3, Pallas kernels, phase(): pl.pallas_call(functools.partial(deblend_kernel, (seg, columns), pieces,...  53.2 us
    ppermute x9, starting transfers between devices, shifted(): return lax.ppermute(shard, axis, pairs)  23.5 us
    ppermute x4, starting transfers between devices, pass_on(): near[k] = lax.ppermute(sent, 'shot', swap)  8.13 us
    pallas_call x4, Pallas kernels, pass_on(): pl.pallas_call(functools.partial(pass_on_kernel, len(ahead) + len(others)...  7.62 us
    ppermute x9, waiting for transfers between devices, shifted(): return lax.ppermute(shard, axis, pairs)  6.87 us
    unnamed x22, local copies, waits for them, and re-layouts  5.49 us
    ppermute x4, waiting for transfers between devices, pass_on(): near[k] = lax.ppermute(sent, 'shot', swap)  3.82 us
    pallas_call x1, Pallas kernels, on_device(): pl.pallas_call(functools.partial(widen_kernel, parts[1:4]), out_shape=tup...  2.56 us
  transfers between devices with their start and end apart: 13, of which 4 were waited for; matrix products, arithmetic and copies ran while one was open for 0% of the time, Pallas kernels for 41%

commit v1 on v0

--- a/solution.py
+++ b/solution.py
@@ -388,8 +388,7 @@
     shots = lax.axis_size("shot")
     q = seg // QUARTERS
     skip = HEAD + 8
-    step = (seg + skip + 4 * 16 - 1) // (4 * 16) * 16
-    parts = [0] + [seg - k * step for k in (3, 2, 1, 0)]
+    parts = [0, 7 * seg // 64, 15 * seg // 32, 47 * seg // 64, seg]
     swap = [(i, i ^ 1) for i in range(shots) if i ^ 1 < shots]
     smem = pl.BlockSpec(memory_space=pltpu.SMEM)
     anywhere = pl.BlockSpec(memory_space=pl.ANY)

time: 119 us -> 118 us (level)
  starting transfers between devices: 31.7 us -> 28.8 us
  waiting for transfers between devices: 10.7 us -> 13.5 us
    ppermute x4, starting transfers between devices: 8.13 us -> 5.13 us  [pass_on(): near[k] = lax.ppermute(sent, 'shot', swap)]
    ppermute x9, waiting for transfers between devices: 6.87 us -> 9.82 us  [shifted(): return lax.ppermute(shard, axis, pairs)]
    unnamed x22 -> x20, local copies, waits for them, and re-layouts: 5.49 us -> 4.7 us
  transfers between devices with their start and end apart: 13 -> 13, of which waited for: 4 -> 5; matrix products, arithmetic and copies ran while one was open for 0% -> 0% of each run, Pallas kernels for 41% -> 41%
where the time goes in v1:
time: 118 us; the launch traced here: 117 us
  Pallas kernels  68.4 us (58%)
  starting transfers between devices  28.8 us (24%)
  waiting for transfers between devices  13.5 us (11%)
  local copies, waits for them, and re-layouts  4.7 us (4%)
  between operations  1.5 us (1%)
    pallas_call x3, Pallas kernels, phase(): pl.pallas_call(functools.partial(deblend_kernel, (seg, columns), pieces,...  53.1 us
    ppermute x9, starting transfers between devices, shifted(): return lax.ppermute(shard, axis, pairs)  23.6 us
    ppermute x9, waiting for transfers between devices, shifted(): return lax.ppermute(shard, axis, pairs)  9.82 us
    pallas_call x4, Pallas kernels, pass_on(): pl.pallas_call(functools.partial(pass_on_kernel, len(ahead) + len(others)...  7.58 us
    ppermute x4, starting transfers between devices, pass_on(): near[k] = lax.ppermute(sent, 'shot', swap)  5.13 us
    unnamed x20, local copies, waits for them, and re-layouts  4.7 us
    ppermute x4, waiting for transfers between devices, pass_on(): near[k] = lax.ppermute(sent, 'shot', swap)  3.68 us
    pallas_call x1, Pallas kernels, on_device(): pl.pallas_call(functools.partial(widen_kernel, parts[1:4]), out_shape=tup...  2.49 us
  transfers between devices with their start and end apart: 13, of which 5 were waited for; matrix products, arithmetic and copies ran while one was open for 0% of the time, Pallas kernels for 41%

profile of v1, /device:TPU:13, one launch (start us, length us, event | category | flops | bytes accessed | tf_op | source)
XLA Modules:
  0.0 116.9 jit_solution(16683100345189625921)
XLA Ops:
  0.0 1.9 %shard_map.64 = (f32[256,128]{1,0:T(8,128)}, f32[256,128]{1,0:T(8,128)}) custom-call(bf16[1024,512]{1,0:T(8,128)(2,1)} %record.1, bf16[1024,512]{1,0:T(8,128)(2,1)} %record.1), custom_call_target="tpu_custom_call" | custom-call | tf_op jit(solution)/shard_map/pallas_call | solution.py:406
  1.9 3.7 %collective-permute-start.1 = (f32[256,128]{1,0:T(8,128)}, f32[256,128]{1,0:T(8,128)S(1)}, u32[]{:S(2)}, u32[]{:S(2)}) collective-permute-start(f32[256,128]{1,0:T(8,128)} %get-tuple-element.17), channel_id=1, source_target_pairs={{0,1},{1,2},{2,3},{4,5},{5,6},{6,7},{8,9},{9,10},{10,11},{12,13},{... | collective-permute-start | bytes 393224 | tf_op jit(solution)/shard_map/ppermute | solution.py:30
  5.5 1.9 %collective-permute-start.2 = (f32[256,128]{1,0:T(8,128)}, f32[256,128]{1,0:T(8,128)S(1)}, u32[]{:S(2)}, u32[]{:S(2)}) collective-permute-start(f32[256,128]{1,0:T(8,128)} %get-tuple-element.18), channel_id=1, source_target_pairs={{1,0},{2,1},{3,2},{5,4},{6,5},{7,6},{9,8},{10,9},{11,10},{13,12},{... | collective-permute-start | bytes 393224 | tf_op jit(solution)/shard_map/ppermute | solution.py:30
  8.8 3.3 %collective-permute-done.2.right = f32[256,128]{1,0:T(8,128)S(1)} collective-permute-done((f32[256,128]{1,0:T(8,128)}, f32[256,128]{1,0:T(8,128)S(1)}, u32[]{:S(2)}, u32[]{:S(2)}) %collective-permute-start.2) | collective-permute-done | bytes 131104 | tf_op jit(solution)/shard_map/ppermute | solution.py:30
  12.0 0.7 copy-done.7
  12.7 1.9 %shard_map.65 = (f32[248,512]{1,0:T(8,128)}, f32[16,768]{1,0:T(8,128)}, f32[24,768]{1,0:T(8,128)}) custom-call(s32[1]{0:T(128)S(6)} %copy.15.offsets, s32[1]{0:T(128)S(6)} %copy.16.lengths, bf16[1024,512]{1,0:T(8,128)(2,1)} %record.1, bf16[1024,512]{1,0:T(8,128)(2,1)} %record.1, f32[256,128]{1,0:T(8,128)} %copy-done.6, f32[256,128]{1,0:T(8,128)} %copy-done.7), custom_call_target="tpu_custom_call" | custom-call | tf_op jit(solution)/shard_map/pallas_call | solution.py:417
  14.6 2.1 %collective-permute-start.4 = (f32[248,512]{1,0:T(8,128)}, f32[248,512]{1,0:T(8,128)S(1)}, u32[]{:S(2)}, u32[]{:S(2)}) collective-permute-start(f32[248,512]{1,0:T(8,128)} %get-tuple-element.20.own.refs_2_.refs_6_), channel_id=1, source_target_pairs={{8,0},{12,4},{16,8},{20,12},{24,16},{28,20},{9,1},{13,5},{17,9},{2... | collective-permute-start | bytes 1523720 | tf_op jit(solution)/shard_map/ppermute | solution.py:30
  16.7 3.1 %collective-permute-start.3 = (f32[24,768]{1,0:T(8,128)}, f32[24,768]{1,0:T(8,128)S(1)}, u32[]{:S(2)}, u32[]{:S(2)}) collective-permute-start(f32[24,768]{1,0:T(8,128)} %get-tuple-element.19), channel_id=1, source_target_pairs={{0,4},{4,8},{8,12},{12,16},{16,20},{20,24},{24,28},{1,5},{5,9},{9,... | collective-permute-start | bytes 221192 | tf_op jit(solution)/shard_map/ppermute | solution.py:30
  19.8 2.4 %collective-permute-done.3.wait.last.refs_6_.refs_13_ = f32[24,768]{1,0:T(8,128)S(1)} collective-permute-done((f32[24,768]{1,0:T(8,128)}, f32[24,768]{1,0:T(8,128)S(1)}, u32[]{:S(2)}, u32[]{:S(2)}) %collective-permute-start.3) | collective-permute-done | bytes 73760 | tf_op jit(solution)/shard_map/ppermute | solution.py:30
  22.3 0.6 copy-done.4
  22.9 2.5 %shard_map.66 = (f32[368,512]{1,0:T(8,128)}, f32[272,512]{1,0:T(8,128)}, f32[272,512]{1,0:T(8,128)}) custom-call(bf16[1024,512]{1,0:T(8,128)(2,1)} %record.1, f32[24,768]{1,0:T(8,128)} %copy-done.4), custom_call_target="tpu_custom_call" | custom-call | tf_op jit(solution)/shard_map/pallas_call | solution.py:431
  25.4 1.9 %collective-permute-start.6 = (f32[368,512]{1,0:T(8,128)}, f32[368,512]{1,0:T(8,128)S(1)}, u32[]{:S(2)}, u32[]{:S(2)}) collective-permute-start(f32[368,512]{1,0:T(8,128)} %get-tuple-element.23.own.refs_3_.refs_7_), channel_id=1, source_target_pairs={{8,0},{12,4},{16,8},{20,12},{24,16},{28,20},{9,1},{13,5},{17,9},{2... | collective-permute-start | bytes 2261000 | tf_op jit(solution)/shard_map/ppermute | solution.py:30
  27.4 0.8 copy-done
  28.2 1.8 %shard_map.67 = (f32[248,512]{1,0:T(8,128)}, f32[272,512]{1,0:T(8,128)}) custom-call(f32[248,512]{1,0:T(8,128)} %get-tuple-element.20.own.refs_2_.refs_6_, f32[248,512]{1,0:T(8,128)} %copy-done, f32[272,512]{1,0:T(8,128)} %get-tuple-element.21.refs_0_), custom_call_target="tpu_custom_call", output_to_operand_aliasing={{1}: (2, {})} | custom-call | tf_op jit(solution)/shard_map/pallas_call | solution.py:441
  30.0 0.8 collective-permute-start.5
  30.8 2.5 %collective-permute-start.7 = (f32[16,768]{1,0:T(8,128)}, f32[16,768]{1,0:T(8,128)S(1)}, u32[]{:S(2)}, u32[]{:S(2)}) collective-permute-start(f32[16,768]{1,0:T(8,128)} %get-tuple-element.25), channel_id=1, source_target_pairs={{12,0},{16,4},{20,8},{24,12},{28,16},{13,1},{17,5},{21,9},{25,13},... | collective-permute-start | bytes 147464 | tf_op jit(solution)/shard_map/ppermute | solution.py:30
  33.5 3.2 %collective-permute-start = (f32[2]{0:T(128)S(1)}, f32[2]{0:T(128)S(1)}, u32[]{:S(2)}, u32[]{:S(2)}) collective-permute-start(f32[2]{0:T(128)S(1)} %add_convert_fusion.mine), channel_id=1, source_target_pairs={{0,8},{4,12},{8,16},{12,20},{16,24},{20,28},{1,9},{5,13},{9,17},{1... | collective-permute-start | bytes 32 | tf_op jit(solution)/shard_map/ppermute | solution.py:30
  36.6 2.1 %collective-permute-start.9 = (f32[272,512]{1,0:T(8,128)}, f32[272,512]{1,0:T(8,128)}, u32[]{:S(2)}, u32[]{:S(2)}) collective-permute-start(f32[272,512]{1,0:T(8,128)} %get-tuple-element.28.refs_4_.own.refs_8_), channel_id=1, source_target_pairs={{8,0},{12,4},{16,8},{20,12},{24,16},{28,20},{9,1},{13,5},{17,9},{2... | collective-permute-start | bytes 1671176 | tf_op jit(solution)/shard_map/ppermute | solution.py:30
  38.8 3.7 %collective-permute-done.5.following.refs_10_.refs_4_ = f32[248,512]{1,0:T(8,128)S(1)} collective-permute-done((f32[248,512]{1,0:T(8,128)}, f32[248,512]{1,0:T(8,128)S(1)}, u32[]{:S(2)}, u32[]{:S(2)}) %collective-permute-start.5) | collective-permute-done | bytes 507936 | tf_op jit(solution)/shard_map/ppermute | solution.py:449
  42.4 0.8 copy-done.2
  43.3 1.4 %shard_map.68.refs_1_.params = s32[8,128]{1,0:T(8,128)} custom-call(f32[2]{0:T(128)} %copy-done.9, f32[24,768]{1,0:T(8,128)} %copy-done.4, f32[2]{0:T(128)} %copy-done.8, f32[248,512]{1,0:T(8,128)} %copy-done.2, f32[248,512]{1,0:T(8,128)} %copy-done), custom_call_target="tpu_custom_call" | custom-call | tf_op jit(solution)/shard_map/pallas_call | solution.py:460
  44.7 4.0 %collective-permute-done.7.refs_2_.refs_12_ = f32[16,768]{1,0:T(8,128)S(1)} collective-permute-done((f32[16,768]{1,0:T(8,128)}, f32[16,768]{1,0:T(8,128)S(1)}, u32[]{:S(2)}, u32[]{:S(2)}) %collective-permute-start.7) | collective-permute-done | bytes 49184 | tf_op jit(solution)/shard_map/ppermute | solution.py:30
  49.6 2.0 %shard_map.69 = (f32[368,512]{1,0:T(8,128)}, f32[272,512]{1,0:T(8,128)}) custom-call(f32[368,512]{1,0:T(8,128)} %get-tuple-element.23.own.refs_3_.refs_7_, f32[368,512]{1,0:T(8,128)} %copy-done.1, f32[272,512]{1,0:T(8,128)} %get-tuple-element.24.refs_0_, s32[8,128]{1,0:T(8,128)} %shard_map.68.refs_1_.params, ...), custom_call_target="tpu_custom_call", output_to_operand_aliasing={{1}: (2, {})} | custom-call | tf_op jit(solution)/shard_map/pallas_call | solution.py:441
  51.6 3.1 %collective-permute-start.11 = (f32[272,512]{1,0:T(8,128)}, f32[272,512]{1,0:T(8,128)}, u32[]{:S(2)}, u32[]{:S(2)}) collective-permute-start(f32[272,512]{1,0:T(8,128)} %get-tuple-element.26.refs_5_.own.refs_9_.refs_3_), channel_id=1, source_target_pairs={{8,0},{12,4},{16,8},{20,12},{24,16},{28,20},{9,1},{13,5},{17,9},{2... | collective-permute-start | bytes 1671176 | tf_op jit(solution)/shard_map/ppermute | solution.py:30
  54.8 11.2 %shard_map.70.refs_0_.refs_15_ = f32[1,2048,512]{2,1,0:T(8,128)} custom-call(s32[8,128]{1,0:T(8,128)} %shard_map.68.refs_1_.params, f32[3]{0:T(128)} %thr.5, bf16[768,640]{1,0:T(8,128)(2,1)} %constant.4.clone.refs_0_, bf16[640,512]{1,0:T(8,128)(2,1)} %constant.5.clone.refs_1_, f32[248,512]{1,0:T(8,128)} %get-tuple-element.20.own.refs_2_.refs_6_, ...), custom_call_target="tpu_custom_call" | custom-call | tf_op jit(solution)/shard_map/pallas_call | solution.py:474
  66.0 1.9 %shard_map.71 = f32[272,512]{1,0:T(8,128)} custom-call(f32[272,512]{1,0:T(8,128)} %get-tuple-element.28.refs_4_.own.refs_8_, f32[272,512]{1,0:T(8,128)} %collective-permute-done.9.far.refs_4_, f32[1,2048,512]{2,1,0:T(8,128)} %shard_map.70.refs_0_.refs_15_), custom_call_target="tpu_custom_call" | custom-call | tf_op jit(solution)/shard_map/pallas_call | solution.py:441
  67.9 2.0 %collective-permute-start.10 = (f32[272,512]{1,0:T(8,128)}, f32[272,512]{1,0:T(8,128)}, u32[]{:S(2)}, u32[]{:S(2)}) collective-permute-start(f32[272,512]{1,0:T(8,128)} %shard_map.71), channel_id=1, source_target_pairs={{0,4},{4,0},{8,12},{12,8},{16,20},{20,16},{24,28},{28,24},{1,5},{5... | collective-permute-start | bytes 1671176 | tf_op jit(solution)/shard_map/ppermute | solution.py:449
  69.9 1.9 %shard_map.72.refs_14_ = f32[272,512]{1,0:T(8,128)} custom-call(f32[272,512]{1,0:T(8,128)} %get-tuple-element.26.refs_5_.own.refs_9_.refs_3_, f32[272,512]{1,0:T(8,128)} %collective-permute-done.11.far.refs_5_), custom_call_target="tpu_custom_call" | custom-call | tf_op jit(solution)/shard_map/pallas_call | solution.py:441
  71.7 2.3 %collective-permute-start.12 = (f32[272,512]{1,0:T(8,128)}, f32[272,512]{1,0:T(8,128)}, u32[]{:S(2)}, u32[]{:S(2)}) collective-permute-start(f32[272,512]{1,0:T(8,128)} %shard_map.72.refs_14_), channel_id=1, source_target_pairs={{0,4},{4,0},{8,12},{12,8},{16,20},{20,16},{24,28},{28,24},{1,5},{5... | collective-permute-start | bytes 1671176 | tf_op jit(solution)/shard_map/ppermute | solution.py:449
  74.1 0.9 copy-done.3
  74.9 25.5 %shard_map.73.refs_10_ = f32[1,2048,512]{2,1,0:T(8,128)} custom-call(s32[8,128]{1,0:T(8,128)} %shard_map.68.refs_1_.params, f32[3]{0:T(128)} %thr.5, bf16[768,640]{1,0:T(8,128)(2,1)} %constant.4.clone.refs_0_, bf16[640,512]{1,0:T(8,128)(2,1)} %constant.5.clone.refs_1_, f32[248,512]{1,0:T(8,128)} %copy-done, ...), custom_call_target="tpu_custom_call", output_to_operand_aliasing={{}: (17, {})} | custom-call | tf_op jit(solution)/shard_map/pallas_call | solution.py:474
  100.5 16.4 %shard_map.74 = f32[1,2048,512]{2,1,0:T(8,128)} custom-call(s32[8,128]{1,0:T(8,128)} %shard_map.68.refs_1_.params, f32[3]{0:T(128)} %thr.5, bf16[768,640]{1,0:T(8,128)(2,1)} %constant.4.clone.refs_0_, bf16[640,512]{1,0:T(8,128)(2,1)} %constant.5.clone.refs_1_, f32[248,512]{1,0:T(8,128)} %get-tuple-element.20.own.refs_2_.refs_6_, ...), custom_call_target="tpu_custom_call", output_to_operand_aliasing={{}: (12, {})} | custom-call | tf_op jit(solution)/shard_map/pallas_call | solution.py:474
  (26 shorter events, 1.2 us)
Async XLA Ops:
  1.9 6.9 %collective-permute-start.1 = (f32[256,128]{1,0:T(8,128)}, f32[256,128]{1,0:T(8,128)S(1)}, u32[]{:S(2)}, u32[]{:S(2)}) collective-permute-start(f32[256,128]{1,0:T(8,128)} %get-tuple-element.17), channel_id=1, source_target_pairs={{0,1},{1,2},{2,3},{4,5},{5,6},{6,7},{8,9},{9,10},{10,11},{12,13},{... | collective-permute-start | bytes 393224 | tf_op jit(solution)/shard_map/ppermute | solution.py:30
  5.5 6.5 %collective-permute-start.2 = (f32[256,128]{1,0:T(8,128)}, f32[256,128]{1,0:T(8,128)S(1)}, u32[]{:S(2)}, u32[]{:S(2)}) collective-permute-start(f32[256,128]{1,0:T(8,128)} %get-tuple-element.18), channel_id=1, source_target_pairs={{1,0},{2,1},{3,2},{5,4},{6,5},{7,6},{9,8},{10,9},{11,10},{13,12},{... | collective-permute-start | bytes 393224 | tf_op jit(solution)/shard_map/ppermute | solution.py:30
  8.8 3.3 %copy-start.6 = (f32[256,128]{1,0:T(8,128)}, f32[256,128]{1,0:T(8,128)S(1)}, u32[]{:S(2)}) copy-start(f32[256,128]{1,0:T(8,128)S(1)} %collective-permute-done.1.left) | copy-start | bytes 393220
  12.0 0.7 copy-start.7
  14.6 12.8 %collective-permute-start.4 = (f32[248,512]{1,0:T(8,128)}, f32[248,512]{1,0:T(8,128)S(1)}, u32[]{:S(2)}, u32[]{:S(2)}) collective-permute-start(f32[248,512]{1,0:T(8,128)} %get-tuple-element.20.own.refs_2_.refs_6_), channel_id=1, source_target_pairs={{8,0},{12,4},{16,8},{20,12},{24,16},{28,20},{9,1},{13,5},{17,9},{2... | collective-permute-start | bytes 1523720 | tf_op jit(solution)/shard_map/ppermute | solution.py:30
  16.7 5.6 %collective-permute-start.3 = (f32[24,768]{1,0:T(8,128)}, f32[24,768]{1,0:T(8,128)S(1)}, u32[]{:S(2)}, u32[]{:S(2)}) collective-permute-start(f32[24,768]{1,0:T(8,128)} %get-tuple-element.19), channel_id=1, source_target_pairs={{0,4},{4,8},{8,12},{12,16},{16,20},{20,24},{24,28},{1,5},{5,9},{9,... | collective-permute-start | bytes 221192 | tf_op jit(solution)/shard_map/ppermute | solution.py:30
  22.3 0.6 copy-start.4
  25.4 23.3 %collective-permute-start.6 = (f32[368,512]{1,0:T(8,128)}, f32[368,512]{1,0:T(8,128)S(1)}, u32[]{:S(2)}, u32[]{:S(2)}) collective-permute-start(f32[368,512]{1,0:T(8,128)} %get-tuple-element.23.own.refs_3_.refs_7_), channel_id=1, source_target_pairs={{8,0},{12,4},{16,8},{20,12},{24,16},{28,20},{9,1},{13,5},{17,9},{2... | collective-permute-start | bytes 2261000 | tf_op jit(solution)/shard_map/ppermute | solution.py:30
  27.4 0.8 copy-start
  30.0 12.4 %collective-permute-start.5 = (f32[248,512]{1,0:T(8,128)}, f32[248,512]{1,0:T(8,128)S(1)}, u32[]{:S(2)}, u32[]{:S(2)}) collective-permute-start(f32[248,512]{1,0:T(8,128)} %get-tuple-element.22), channel_id=1, source_target_pairs={{0,4},{4,0},{8,12},{12,8},{16,20},{20,16},{24,28},{28,24},{1,5},{5... | collective-permute-start | bytes 1523720 | tf_op jit(solution)/shard_map/ppermute | solution.py:449
  30.8 17.8 %collective-permute-start.7 = (f32[16,768]{1,0:T(8,128)}, f32[16,768]{1,0:T(8,128)S(1)}, u32[]{:S(2)}, u32[]{:S(2)}) collective-permute-start(f32[16,768]{1,0:T(8,128)} %get-tuple-element.25), channel_id=1, source_target_pairs={{12,0},{16,4},{20,8},{24,12},{28,16},{13,1},{17,5},{21,9},{25,13},... | collective-permute-start | bytes 147464 | tf_op jit(solution)/shard_map/ppermute | solution.py:30
  33.4 9.0 %copy-start.8 = (f32[2]{0:T(128)}, f32[2]{0:T(128)S(1)}, u32[]{:S(2)}) copy-start(f32[2]{0:T(128)S(1)} %add_convert_fusion.mine) | copy-start | bytes 28
  33.5 5.3 %collective-permute-start = (f32[2]{0:T(128)S(1)}, f32[2]{0:T(128)S(1)}, u32[]{:S(2)}, u32[]{:S(2)}) collective-permute-start(f32[2]{0:T(128)S(1)} %add_convert_fusion.mine), channel_id=1, source_target_pairs={{0,8},{4,12},{8,16},{12,20},{16,24},{20,28},{1,9},{5,13},{9,17},{1... | collective-permute-start | bytes 32 | tf_op jit(solution)/shard_map/ppermute | solution.py:30
  36.6 29.3 %collective-permute-start.9 = (f32[272,512]{1,0:T(8,128)}, f32[272,512]{1,0:T(8,128)}, u32[]{:S(2)}, u32[]{:S(2)}) collective-permute-start(f32[272,512]{1,0:T(8,128)} %get-tuple-element.28.refs_4_.own.refs_8_), channel_id=1, source_target_pairs={{8,0},{12,4},{16,8},{20,12},{24,16},{28,20},{9,1},{13,5},{17,9},{2... | collective-permute-start | bytes 1671176 | tf_op jit(solution)/shard_map/ppermute | solution.py:30
  38.7 3.7 %copy-start.9 = (f32[2]{0:T(128)}, f32[2]{0:T(128)S(1)}, u32[]{:S(2)}) copy-start(f32[2]{0:T(128)S(1)} %collective-permute-done.second_last) | copy-start | bytes 28
  42.4 0.8 copy-start.2
  48.7 0.6 copy-start.5
  48.7 0.9 copy-start.1
  51.6 18.3 %collective-permute-start.11 = (f32[272,512]{1,0:T(8,128)}, f32[272,512]{1,0:T(8,128)}, u32[]{:S(2)}, u32[]{:S(2)}) collective-permute-start(f32[272,512]{1,0:T(8,128)} %get-tuple-element.26.refs_5_.own.refs_9_.refs_3_), channel_id=1, source_target_pairs={{8,0},{12,4},{16,8},{20,12},{24,16},{28,20},{9,1},{13,5},{17,9},{2... | collective-permute-start | bytes 1671176 | tf_op jit(solution)/shard_map/ppermute | solution.py:30
  54.7 19.3 %collective-permute-start.8 = (f32[368,512]{1,0:T(8,128)}, f32[368,512]{1,0:T(8,128)S(1)}, u32[]{:S(2)}, u32[]{:S(2)}) collective-permute-start(f32[368,512]{1,0:T(8,128)} %get-tuple-element.27), channel_id=1, source_target_pairs={{0,4},{4,0},{8,12},{12,8},{16,20},{20,16},{24,28},{28,24},{1,5},{5... | collective-permute-start | bytes 2261000 | tf_op jit(solution)/shard_map/ppermute | solution.py:449
  67.9 32.6 %collective-permute-start.10 = (f32[272,512]{1,0:T(8,128)}, f32[272,512]{1,0:T(8,128)}, u32[]{:S(2)}, u32[]{:S(2)}) collective-permute-start(f32[272,512]{1,0:T(8,128)} %shard_map.71), channel_id=1, source_target_pairs={{0,4},{4,0},{8,12},{12,8},{16,20},{20,16},{24,28},{28,24},{1,5},{5... | collective-permute-start | bytes 1671176 | tf_op jit(solution)/shard_map/ppermute | solution.py:449
  71.7 28.7 %collective-permute-start.12 = (f32[272,512]{1,0:T(8,128)}, f32[272,512]{1,0:T(8,128)}, u32[]{:S(2)}, u32[]{:S(2)}) collective-permute-start(f32[272,512]{1,0:T(8,128)} %shard_map.72.refs_14_), channel_id=1, source_target_pairs={{0,4},{4,0},{8,12},{12,8},{16,20},{20,16},{24,28},{28,24},{1,5},{5... | collective-permute-start | bytes 1671176 | tf_op jit(solution)/shard_map/ppermute | solution.py:449
  74.1 0.9 copy-start.3

commit v2 on v1

--- a/solution.py
+++ b/solution.py
@@ -120,7 +120,11 @@
     def shot(by):
         return by * seg + params[by + 2, 0] - offset, params[by + 2, 1]
 
-    spans = [(pl.multiple_of(begin * BLOCK, 8), jnp.maximum(end - begin, 0)) for begin, end in span(offset)]
+    live_blocks = (live + BLOCK - 1) // BLOCK
+    whole = [(begin, jnp.maximum(end, begin)) for begin, end in span(offset)]
+    spans = [
+        (pl.multiple_of(begin * BLOCK, 8), jnp.maximum(jnp.minimum(end, live_blocks) - begin, 0)) for begin, end in whole
+    ]
     some = sum(count for _, count in spans) > 0
 
     def reached(row, rows):
@@ -320,8 +324,15 @@
         out_copy(i).wait()
         return carry
 
-    for low, count in spans:
-        lax.fori_loop(low // BLOCK, low // BLOCK + count, wait, 0)
+    def clear(i, carry):
+        staged[pl.ds(pl.multiple_of(i * BLOCK, BLOCK), BLOCK), :] = jnp.zeros((BLOCK, columns), jnp.float32)
+        out_copy(i).start()
+        return carry
+
+    for begin, end in whole:
+        lax.fori_loop(jnp.maximum(begin, live_blocks), end, clear, 0)
+    for begin, end in whole:
+        lax.fori_loop(begin, end, wait, 0)
 
 
 def prepare_kernel(first_columns, last_columns, first_edge, last_edge):

time: 118 us -> 118 us (level)
  the two profiles are of different devices: /device:TPU:13 before, /device:TPU:1 now
where the time goes in v2:
time: 118 us; the launch traced here: 117 us
  Pallas kernels  64.9 us (55%)
  starting transfers between devices  29.8 us (25%)
  waiting for transfers between devices  15.7 us (13%)
  local copies, waits for them, and re-layouts  4.7 us (4%)
  between operations  1.49 us (1%)
    pallas_call x3, Pallas kernels, phase(): pl.pallas_call(functools.partial(deblend_kernel, (seg, columns), pieces,...  49.7 us
    ppermute x9, starting transfers between devices, shifted(): return lax.ppermute(shard, axis, pairs)  19.2 us
    ppermute x4, starting transfers between devices, pass_on(): near[k] = lax.ppermute(sent, 'shot', swap)  10.6 us
    ppermute x9, waiting for transfers between devices, shifted(): return lax.ppermute(shard, axis, pairs)  10.5 us
    pallas_call x4, Pallas kernels, pass_on(): pl.pallas_call(functools.partial(pass_on_kernel, len(ahead) + len(others)...  7.58 us
    ppermute x4, waiting for transfers between devices, pass_on(): near[k] = lax.ppermute(sent, 'shot', swap)  5.2 us
    unnamed x20, local copies, waits for them, and re-layouts  4.7 us
    pallas_call x1, Pallas kernels, on_device(): pl.pallas_call(functools.partial(widen_kernel, parts[1:4]), out_shape=tup...  2.49 us
  transfers between devices with their start and end apart: 13, of which 5 were waited for; matrix products, arithmetic and copies ran while one was open for 0% of the time, Pallas kernels for 39%

profile of v2, /device:TPU:1, one launch (start us, length us, event | category | flops | bytes accessed | tf_op | source)
XLA Modules:
  0.0 116.7 jit_solution(378913395112846892)
XLA Ops:
  0.0 1.9 %shard_map.64 = (f32[256,128]{1,0:T(8,128)}, f32[256,128]{1,0:T(8,128)}) custom-call(bf16[1024,512]{1,0:T(8,128)(2,1)} %record.1, bf16[1024,512]{1,0:T(8,128)(2,1)} %record.1), custom_call_target="tpu_custom_call" | custom-call | tf_op jit(solution)/shard_map/pallas_call | solution.py:417
  1.9 4.5 %collective-permute-start.1 = (f32[256,128]{1,0:T(8,128)}, f32[256,128]{1,0:T(8,128)S(1)}, u32[]{:S(2)}, u32[]{:S(2)}) collective-permute-start(f32[256,128]{1,0:T(8,128)} %get-tuple-element.17), channel_id=1, source_target_pairs={{0,1},{1,2},{2,3},{4,5},{5,6},{6,7},{8,9},{9,10},{10,11},{12,13},{... | collective-permute-start | bytes 393224 | tf_op jit(solution)/shard_map/ppermute | solution.py:30
  6.4 1.9 %collective-permute-start.2 = (f32[256,128]{1,0:T(8,128)}, f32[256,128]{1,0:T(8,128)S(1)}, u32[]{:S(2)}, u32[]{:S(2)}) collective-permute-start(f32[256,128]{1,0:T(8,128)} %get-tuple-element.18), channel_id=1, source_target_pairs={{1,0},{2,1},{3,2},{5,4},{6,5},{7,6},{9,8},{10,9},{11,10},{13,12},{... | collective-permute-start | bytes 393224 | tf_op jit(solution)/shard_map/ppermute | solution.py:30
  9.6 3.3 %collective-permute-done.2.right = f32[256,128]{1,0:T(8,128)S(1)} collective-permute-done((f32[256,128]{1,0:T(8,128)}, f32[256,128]{1,0:T(8,128)S(1)}, u32[]{:S(2)}, u32[]{:S(2)}) %collective-permute-start.2) | collective-permute-done | bytes 131104 | tf_op jit(solution)/shard_map/ppermute | solution.py:30
  12.9 0.7 copy-done.7
  13.5 1.9 %shard_map.65 = (f32[248,512]{1,0:T(8,128)}, f32[16,768]{1,0:T(8,128)}, f32[24,768]{1,0:T(8,128)}) custom-call(s32[1]{0:T(128)S(6)} %copy.15.offsets, s32[1]{0:T(128)S(6)} %copy.16.lengths, bf16[1024,512]{1,0:T(8,128)(2,1)} %record.1, bf16[1024,512]{1,0:T(8,128)(2,1)} %record.1, f32[256,128]{1,0:T(8,128)} %copy-done.6, f32[256,128]{1,0:T(8,128)} %copy-done.7), custom_call_target="tpu_custom_call" | custom-call | tf_op jit(solution)/shard_map/pallas_call | solution.py:428
  15.4 1.3 %collective-permute-start.4 = (f32[248,512]{1,0:T(8,128)}, f32[248,512]{1,0:T(8,128)S(1)}, u32[]{:S(2)}, u32[]{:S(2)}) collective-permute-start(f32[248,512]{1,0:T(8,128)} %get-tuple-element.20.own.refs_2_.refs_6_), channel_id=1, source_target_pairs={{8,0},{12,4},{16,8},{20,12},{24,16},{28,20},{9,1},{13,5},{17,9},{2... | collective-permute-start | bytes 1523720 | tf_op jit(solution)/shard_map/ppermute | solution.py:30
  16.7 3.1 %collective-permute-start.3 = (f32[24,768]{1,0:T(8,128)}, f32[24,768]{1,0:T(8,128)S(1)}, u32[]{:S(2)}, u32[]{:S(2)}) collective-permute-start(f32[24,768]{1,0:T(8,128)} %get-tuple-element.19), channel_id=1, source_target_pairs={{0,4},{4,8},{8,12},{12,16},{16,20},{20,24},{24,28},{1,5},{5,9},{9,... | collective-permute-start | bytes 221192 | tf_op jit(solution)/shard_map/ppermute | solution.py:30
  19.9 1.7 %collective-permute-done.3.wait.last.refs_6_.refs_13_ = f32[24,768]{1,0:T(8,128)S(1)} collective-permute-done((f32[24,768]{1,0:T(8,128)}, f32[24,768]{1,0:T(8,128)S(1)}, u32[]{:S(2)}, u32[]{:S(2)}) %collective-permute-start.3) | collective-permute-done | bytes 73760 | tf_op jit(solution)/shard_map/ppermute | solution.py:30
  22.2 2.5 %shard_map.66 = (f32[368,512]{1,0:T(8,128)}, f32[272,512]{1,0:T(8,128)}, f32[272,512]{1,0:T(8,128)}) custom-call(bf16[1024,512]{1,0:T(8,128)(2,1)} %record.1, f32[24,768]{1,0:T(8,128)} %copy-done.4), custom_call_target="tpu_custom_call" | custom-call | tf_op jit(solution)/shard_map/pallas_call | solution.py:442
  24.7 1.3 %collective-permute-start.6 = (f32[368,512]{1,0:T(8,128)}, f32[368,512]{1,0:T(8,128)S(1)}, u32[]{:S(2)}, u32[]{:S(2)}) collective-permute-start(f32[368,512]{1,0:T(8,128)} %get-tuple-element.23.own.refs_3_.refs_7_), channel_id=1, source_target_pairs={{8,0},{12,4},{16,8},{20,12},{24,16},{28,20},{9,1},{13,5},{17,9},{2... | collective-permute-start | bytes 2261000 | tf_op jit(solution)/shard_map/ppermute | solution.py:30
  26.0 2.3 %collective-permute-done.4.far.second.refs_7_.refs_2_.refs_8_ = f32[248,512]{1,0:T(8,128)S(1)} collective-permute-done((f32[248,512]{1,0:T(8,128)}, f32[248,512]{1,0:T(8,128)S(1)}, u32[]{:S(2)}, u32[]{:S(2)}) %collective-permute-start.4) | collective-permute-done | bytes 507936 | tf_op jit(solution)/shard_map/ppermute | solution.py:30
  28.3 0.8 copy-done
  29.0 1.8 %shard_map.67 = (f32[248,512]{1,0:T(8,128)}, f32[272,512]{1,0:T(8,128)}) custom-call(f32[248,512]{1,0:T(8,128)} %get-tuple-element.20.own.refs_2_.refs_6_, f32[248,512]{1,0:T(8,128)} %copy-done, f32[272,512]{1,0:T(8,128)} %get-tuple-element.21.refs_0_), custom_call_target="tpu_custom_call", output_to_operand_aliasing={{1}: (2, {})} | custom-call | tf_op jit(solution)/shard_map/pallas_call | solution.py:452
  30.9 1.3 %collective-permute-start.5 = (f32[248,512]{1,0:T(8,128)}, f32[248,512]{1,0:T(8,128)S(1)}, u32[]{:S(2)}, u32[]{:S(2)}) collective-permute-start(f32[248,512]{1,0:T(8,128)} %get-tuple-element.22), channel_id=1, source_target_pairs={{0,4},{4,0},{8,12},{12,8},{16,20},{20,16},{24,28},{28,24},{1,5},{5... | collective-permute-start | bytes 1523720 | tf_op jit(solution)/shard_map/ppermute | solution.py:460
  32.2 1.3 %collective-permute-start.7 = (f32[16,768]{1,0:T(8,128)}, f32[16,768]{1,0:T(8,128)S(1)}, u32[]{:S(2)}, u32[]{:S(2)}) collective-permute-start(f32[16,768]{1,0:T(8,128)} %get-tuple-element.25), channel_id=1, source_target_pairs={{12,0},{16,4},{20,8},{24,12},{28,16},{13,1},{17,5},{21,9},{25,13},... | collective-permute-start | bytes 147464 | tf_op jit(solution)/shard_map/ppermute | solution.py:30
  33.6 3.2 %collective-permute-start = (f32[2]{0:T(128)S(1)}, f32[2]{0:T(128)S(1)}, u32[]{:S(2)}, u32[]{:S(2)}) collective-permute-start(f32[2]{0:T(128)S(1)} %add_convert_fusion.mine), channel_id=1, source_target_pairs={{0,8},{4,12},{8,16},{12,20},{16,24},{20,28},{1,9},{5,13},{9,17},{1... | collective-permute-start | bytes 32 | tf_op jit(solution)/shard_map/ppermute | solution.py:30
  36.7 1.3 %collective-permute-start.9 = (f32[272,512]{1,0:T(8,128)}, f32[272,512]{1,0:T(8,128)}, u32[]{:S(2)}, u32[]{:S(2)}) collective-permute-start(f32[272,512]{1,0:T(8,128)} %get-tuple-element.28.refs_4_.own.refs_8_), channel_id=1, source_target_pairs={{8,0},{12,4},{16,8},{20,12},{24,16},{28,20},{9,1},{13,5},{17,9},{2... | collective-permute-start | bytes 1671176 | tf_op jit(solution)/shard_map/ppermute | solution.py:30
  38.1 5.2 %collective-permute-done.5.following.refs_10_.refs_4_ = f32[248,512]{1,0:T(8,128)S(1)} collective-permute-done((f32[248,512]{1,0:T(8,128)}, f32[248,512]{1,0:T(8,128)S(1)}, u32[]{:S(2)}, u32[]{:S(2)}) %collective-permute-start.5) | collective-permute-done | bytes 507936 | tf_op jit(solution)/shard_map/ppermute | solution.py:460
  43.3 0.8 copy-done.2
  44.1 1.4 %shard_map.68.refs_1_.params = s32[8,128]{1,0:T(8,128)} custom-call(f32[2]{0:T(128)} %copy-done.9, f32[24,768]{1,0:T(8,128)} %copy-done.4, f32[2]{0:T(128)} %copy-done.8, f32[248,512]{1,0:T(8,128)} %copy-done.2, f32[248,512]{1,0:T(8,128)} %copy-done), custom_call_target="tpu_custom_call" | custom-call | tf_op jit(solution)/shard_map/pallas_call | solution.py:471
  45.5 3.3 %collective-permute-done.7.refs_2_.refs_12_ = f32[16,768]{1,0:T(8,128)S(1)} collective-permute-done((f32[16,768]{1,0:T(8,128)}, f32[16,768]{1,0:T(8,128)S(1)}, u32[]{:S(2)}, u32[]{:S(2)}) %collective-permute-start.7) | collective-permute-done | bytes 49184 | tf_op jit(solution)/shard_map/ppermute | solution.py:30
  49.7 2.0 %shard_map.69 = (f32[368,512]{1,0:T(8,128)}, f32[272,512]{1,0:T(8,128)}) custom-call(f32[368,512]{1,0:T(8,128)} %get-tuple-element.23.own.refs_3_.refs_7_, f32[368,512]{1,0:T(8,128)} %copy-done.1, f32[272,512]{1,0:T(8,128)} %get-tuple-element.24.refs_0_, s32[8,128]{1,0:T(8,128)} %shard_map.68.refs_1_.params, ...), custom_call_target="tpu_custom_call", output_to_operand_aliasing={{1}: (2, {})} | custom-call | tf_op jit(solution)/shard_map/pallas_call | solution.py:452
  51.7 1.3 %collective-permute-start.11 = (f32[272,512]{1,0:T(8,128)}, f32[272,512]{1,0:T(8,128)}, u32[]{:S(2)}, u32[]{:S(2)}) collective-permute-start(f32[272,512]{1,0:T(8,128)} %get-tuple-element.26.refs_5_.own.refs_9_.refs_3_), channel_id=1, source_target_pairs={{8,0},{12,4},{16,8},{20,12},{24,16},{28,20},{9,1},{13,5},{17,9},{2... | collective-permute-start | bytes 1671176 | tf_op jit(solution)/shard_map/ppermute | solution.py:30
  53.0 3.1 %collective-permute-start.8 = (f32[368,512]{1,0:T(8,128)}, f32[368,512]{1,0:T(8,128)S(1)}, u32[]{:S(2)}, u32[]{:S(2)}) collective-permute-start(f32[368,512]{1,0:T(8,128)} %get-tuple-element.27), channel_id=1, source_target_pairs={{0,4},{4,0},{8,12},{12,8},{16,20},{20,16},{24,28},{28,24},{1,5},{5... | collective-permute-start | bytes 2261000 | tf_op jit(solution)/shard_map/ppermute | solution.py:460
  56.1 8.5 %shard_map.70.refs_0_.refs_15_ = f32[1,2048,512]{2,1,0:T(8,128)} custom-call(s32[8,128]{1,0:T(8,128)} %shard_map.68.refs_1_.params, f32[3]{0:T(128)} %thr.5, bf16[768,640]{1,0:T(8,128)(2,1)} %constant.4.clone.refs_0_, bf16[640,512]{1,0:T(8,128)(2,1)} %constant.5.clone.refs_1_, f32[248,512]{1,0:T(8,128)} %get-tuple-element.20.own.refs_2_.refs_6_, ...), custom_call_target="tpu_custom_call" | custom-call | tf_op jit(solution)/shard_map/pallas_call | solution.py:485
  64.6 1.9 %shard_map.71 = f32[272,512]{1,0:T(8,128)} custom-call(f32[272,512]{1,0:T(8,128)} %get-tuple-element.28.refs_4_.own.refs_8_, f32[272,512]{1,0:T(8,128)} %collective-permute-done.9.far.refs_4_, f32[1,2048,512]{2,1,0:T(8,128)} %shard_map.70.refs_0_.refs_15_), custom_call_target="tpu_custom_call" | custom-call | tf_op jit(solution)/shard_map/pallas_call | solution.py:452
  66.5 6.1 %collective-permute-start.10 = (f32[272,512]{1,0:T(8,128)}, f32[272,512]{1,0:T(8,128)}, u32[]{:S(2)}, u32[]{:S(2)}) collective-permute-start(f32[272,512]{1,0:T(8,128)} %shard_map.71), channel_id=1, source_target_pairs={{0,4},{4,0},{8,12},{12,8},{16,20},{20,16},{24,28},{28,24},{1,5},{5... | collective-permute-start | bytes 1671176 | tf_op jit(solution)/shard_map/ppermute | solution.py:460
  72.6 1.9 %shard_map.72.refs_14_ = f32[272,512]{1,0:T(8,128)} custom-call(f32[272,512]{1,0:T(8,128)} %get-tuple-element.26.refs_5_.own.refs_9_.refs_3_, f32[272,512]{1,0:T(8,128)} %collective-permute-done.11.far.refs_5_), custom_call_target="tpu_custom_call" | custom-call | tf_op jit(solution)/shard_map/pallas_call | solution.py:452
  74.6 0.9 copy-done.3
  75.5 25.6 %shard_map.73.refs_10_ = f32[1,2048,512]{2,1,0:T(8,128)} custom-call(s32[8,128]{1,0:T(8,128)} %shard_map.68.refs_1_.params, f32[3]{0:T(128)} %thr.5, bf16[768,640]{1,0:T(8,128)(2,1)} %constant.4.clone.refs_0_, bf16[640,512]{1,0:T(8,128)(2,1)} %constant.5.clone.refs_1_, f32[248,512]{1,0:T(8,128)} %copy-done, ...), custom_call_target="tpu_custom_call", output_to_operand_aliasing={{}: (17, {})} | custom-call | tf_op jit(solution)/shard_map/pallas_call | solution.py:485
  101.1 15.6 %shard_map.74 = f32[1,2048,512]{2,1,0:T(8,128)} custom-call(s32[8,128]{1,0:T(8,128)} %shard_map.68.refs_1_.params, f32[3]{0:T(128)} %thr.5, bf16[768,640]{1,0:T(8,128)(2,1)} %constant.4.clone.refs_0_, bf16[640,512]{1,0:T(8,128)(2,1)} %constant.5.clone.refs_1_, f32[248,512]{1,0:T(8,128)} %get-tuple-element.20.own.refs_2_.refs_6_, ...), custom_call_target="tpu_custom_call", output_to_operand_aliasing={{}: (12, {})} | custom-call | tf_op jit(solution)/shard_map/pallas_call | solution.py:485
  (26 shorter events, 1.8 us)
Async XLA Ops:
  1.9 7.7 %collective-permute-start.1 = (f32[256,128]{1,0:T(8,128)}, f32[256,128]{1,0:T(8,128)S(1)}, u32[]{:S(2)}, u32[]{:S(2)}) collective-permute-start(f32[256,128]{1,0:T(8,128)} %get-tuple-element.17), channel_id=1, source_target_pairs={{0,1},{1,2},{2,3},{4,5},{5,6},{6,7},{8,9},{9,10},{10,11},{12,13},{... | collective-permute-start | bytes 393224 | tf_op jit(solution)/shard_map/ppermute | solution.py:30
  6.4 6.5 %collective-permute-start.2 = (f32[256,128]{1,0:T(8,128)}, f32[256,128]{1,0:T(8,128)S(1)}, u32[]{:S(2)}, u32[]{:S(2)}) collective-permute-start(f32[256,128]{1,0:T(8,128)} %get-tuple-element.18), channel_id=1, source_target_pairs={{1,0},{2,1},{3,2},{5,4},{6,5},{7,6},{9,8},{10,9},{11,10},{13,12},{... | collective-permute-start | bytes 393224 | tf_op jit(solution)/shard_map/ppermute | solution.py:30
  9.6 3.3 %copy-start.6 = (f32[256,128]{1,0:T(8,128)}, f32[256,128]{1,0:T(8,128)S(1)}, u32[]{:S(2)}) copy-start(f32[256,128]{1,0:T(8,128)S(1)} %collective-permute-done.1.left) | copy-start | bytes 393220
  12.9 0.7 copy-start.7
  15.4 12.8 %collective-permute-start.4 = (f32[248,512]{1,0:T(8,128)}, f32[248,512]{1,0:T(8,128)S(1)}, u32[]{:S(2)}, u32[]{:S(2)}) collective-permute-start(f32[248,512]{1,0:T(8,128)} %get-tuple-element.20.own.refs_2_.refs_6_), channel_id=1, source_target_pairs={{8,0},{12,4},{16,8},{20,12},{24,16},{28,20},{9,1},{13,5},{17,9},{2... | collective-permute-start | bytes 1523720 | tf_op jit(solution)/shard_map/ppermute | solution.py:30
  16.7 4.9 %collective-permute-start.3 = (f32[24,768]{1,0:T(8,128)}, f32[24,768]{1,0:T(8,128)S(1)}, u32[]{:S(2)}, u32[]{:S(2)}) collective-permute-start(f32[24,768]{1,0:T(8,128)} %get-tuple-element.19), channel_id=1, source_target_pairs={{0,4},{4,8},{8,12},{12,16},{16,20},{20,24},{24,28},{1,5},{5,9},{9,... | collective-permute-start | bytes 221192 | tf_op jit(solution)/shard_map/ppermute | solution.py:30
  21.6 0.6 copy-start.4
  24.7 24.1 %collective-permute-start.6 = (f32[368,512]{1,0:T(8,128)}, f32[368,512]{1,0:T(8,128)S(1)}, u32[]{:S(2)}, u32[]{:S(2)}) collective-permute-start(f32[368,512]{1,0:T(8,128)} %get-tuple-element.23.own.refs_3_.refs_7_), channel_id=1, source_target_pairs={{8,0},{12,4},{16,8},{20,12},{24,16},{28,20},{9,1},{13,5},{17,9},{2... | collective-permute-start | bytes 2261000 | tf_op jit(solution)/shard_map/ppermute | solution.py:30
  28.2 0.8 copy-start
  30.9 12.4 %collective-permute-start.5 = (f32[248,512]{1,0:T(8,128)}, f32[248,512]{1,0:T(8,128)S(1)}, u32[]{:S(2)}, u32[]{:S(2)}) collective-permute-start(f32[248,512]{1,0:T(8,128)} %get-tuple-element.22), channel_id=1, source_target_pairs={{0,4},{4,0},{8,12},{12,8},{16,20},{20,16},{24,28},{28,24},{1,5},{5... | collective-permute-start | bytes 1523720 | tf_op jit(solution)/shard_map/ppermute | solution.py:460
  32.2 16.6 %collective-permute-start.7 = (f32[16,768]{1,0:T(8,128)}, f32[16,768]{1,0:T(8,128)S(1)}, u32[]{:S(2)}, u32[]{:S(2)}) collective-permute-start(f32[16,768]{1,0:T(8,128)} %get-tuple-element.25), channel_id=1, source_target_pairs={{12,0},{16,4},{20,8},{24,12},{28,16},{13,1},{17,5},{21,9},{25,13},... | collective-permute-start | bytes 147464 | tf_op jit(solution)/shard_map/ppermute | solution.py:30
  33.5 9.7 %copy-start.8 = (f32[2]{0:T(128)}, f32[2]{0:T(128)S(1)}, u32[]{:S(2)}) copy-start(f32[2]{0:T(128)S(1)} %add_convert_fusion.mine) | copy-start | bytes 28
  33.6 4.5 %collective-permute-start = (f32[2]{0:T(128)S(1)}, f32[2]{0:T(128)S(1)}, u32[]{:S(2)}, u32[]{:S(2)}) collective-permute-start(f32[2]{0:T(128)S(1)} %add_convert_fusion.mine), channel_id=1, source_target_pairs={{0,8},{4,12},{8,16},{12,20},{16,24},{20,28},{1,9},{5,13},{9,17},{1... | collective-permute-start | bytes 32 | tf_op jit(solution)/shard_map/ppermute | solution.py:30
  36.7 27.8 %collective-permute-start.9 = (f32[272,512]{1,0:T(8,128)}, f32[272,512]{1,0:T(8,128)}, u32[]{:S(2)}, u32[]{:S(2)}) collective-permute-start(f32[272,512]{1,0:T(8,128)} %get-tuple-element.28.refs_4_.own.refs_8_), channel_id=1, source_target_pairs={{8,0},{12,4},{16,8},{20,12},{24,16},{28,20},{9,1},{13,5},{17,9},{2... | collective-permute-start | bytes 1671176 | tf_op jit(solution)/shard_map/ppermute | solution.py:30
  38.1 5.2 %copy-start.9 = (f32[2]{0:T(128)}, f32[2]{0:T(128)S(1)}, u32[]{:S(2)}) copy-start(f32[2]{0:T(128)S(1)} %collective-permute-done.second_last) | copy-start | bytes 28
  43.3 0.8 copy-start.2
  48.8 0.6 copy-start.5
  48.8 0.9 copy-start.1
  51.7 20.9 %collective-permute-start.11 = (f32[272,512]{1,0:T(8,128)}, f32[272,512]{1,0:T(8,128)}, u32[]{:S(2)}, u32[]{:S(2)}) collective-permute-start(f32[272,512]{1,0:T(8,128)} %get-tuple-element.26.refs_5_.own.refs_9_.refs_3_), channel_id=1, source_target_pairs={{8,0},{12,4},{16,8},{20,12},{24,16},{28,20},{9,1},{13,5},{17,9},{2... | collective-permute-start | bytes 1671176 | tf_op jit(solution)/shard_map/ppermute | solution.py:30
  53.0 21.6 %collective-permute-start.8 = (f32[368,512]{1,0:T(8,128)}, f32[368,512]{1,0:T(8,128)S(1)}, u32[]{:S(2)}, u32[]{:S(2)}) collective-permute-start(f32[368,512]{1,0:T(8,128)} %get-tuple-element.27), channel_id=1, source_target_pairs={{0,4},{4,0},{8,12},{12,8},{16,20},{20,16},{24,28},{28,24},{1,5},{5... | collective-permute-start | bytes 2261000 | tf_op jit(solution)/shard_map/ppermute | solution.py:460
  66.5 34.6 %collective-permute-start.10 = (f32[272,512]{1,0:T(8,128)}, f32[272,512]{1,0:T(8,128)}, u32[]{:S(2)}, u32[]{:S(2)}) collective-permute-start(f32[272,512]{1,0:T(8,128)} %shard_map.71), channel_id=1, source_target_pairs={{0,4},{4,0},{8,12},{12,8},{16,20},{20,16},{24,28},{28,24},{1,5},{5... | collective-permute-start | bytes 1671176 | tf_op jit(solution)/shard_map/ppermute | solution.py:460
  74.5 26.6 %collective-permute-start.12 = (f32[272,512]{1,0:T(8,128)}, f32[272,512]{1,0:T(8,128)}, u32[]{:S(2)}, u32[]{:S(2)}) collective-permute-start(f32[272,512]{1,0:T(8,128)} %shard_map.72.refs_14_), channel_id=1, source_target_pairs={{0,4},{4,0},{8,12},{12,8},{16,20},{20,16},{24,28},{28,24},{1,5},{5... | collective-permute-start | bytes 1671176 | tf_op jit(solution)/shard_map/ppermute | solution.py:460
  74.6 0.9 copy-start.3
